TPU v7x, 256 devices: a whole 4x4x8 slice. The times are simulated.
256 devices in a mesh: grp: 4 (over y), row: 8 (over z), col: 8 (over x, core).
Axes of the slice: x: 4, y: 4, z: 8, core: 2. Of those that a mesh axis runs over, the one named last changes fastest.
Arguments:
- front: float32 [4, 8, 8, 8, 8, 128, 128], P('grp', 'row', None, 'col'), as said below
- child_update: float32 [4, 2, 8, 5, 8, 5, 128, 128], P('grp', None, 'row', None, 'col'), as said below
- child_tiles: int32 [4, 2, 40], replicated, may hold values from 0 to 63, as said below
Outputs:
- factored: float32 [4, 8, 8, 8, 8, 128, 128], P('grp', 'row', None, 'col')
Inputs may be any that keep to these rules, and one draw needn't show every extreme that they name: `child_tiles`: each list holds 40 distinct front tiles in increasing order, exactly 5 of them of each residue modulo 8. `child_update`: each child update is a symmetric matrix over its listed tiles. Each front is symmetric, and with its children added the leading 5 * 128 square block is positive definite.
All inputs are finite; a program needn't handle non-finite values.
Results may differ from a plain program's by a relative error of at most 0.0001.
Values sent between devices are 32-bit elements; how exact they have to be, the bound alone decides.
No kernel may reach another device: no remote copies, remote signals or barrier semaphores. Data moves between devices by JAX's collectives and lax.ppermute only.
A program may use at most 128 MiB of HBM per device.

v0:
```python
import functools

import jax
import jax.numpy as jnp
from jax import lax
from jax.experimental import pallas as pl
from jax.experimental.pallas import tpu as pltpu
from jax.sharding import PartitionSpec as P

PANELS = 5
TILE = 128
LEAD = PANELS * TILE
BLOCK = 32
SUB = 16
SLOTS = 3
HEAD = 3
WIDTH = 2
CUTS = ((0, 256), (256, 512), (512, 640))
HIGHEST = lax.Precision.HIGHEST
VMEM = pltpu.VMEM
SMEM = pltpu.SMEM


def mul_nn(a, b, precision=HIGHEST):
    return lax.dot_general(
        a, b, (((1,), (0,)), ((), ())), precision=precision, preferred_element_type=jnp.float32
    )


def mul_tn(a, b, precision=HIGHEST):
    return lax.dot_general(
        a, b, (((0,), (0,)), ((), ())), precision=precision, preferred_element_type=jnp.float32
    )


def mul_nt(a, b, precision=HIGHEST):
    return lax.dot_general(
        a, b, (((1,), (1,)), ((), ())), precision=precision, preferred_element_type=jnp.float32
    )


def over_rows(x, at):
    return jnp.broadcast_to(x[at : at + 1, :], (8, TILE))


def eliminate(v, w, base):
    parts = BLOCK // 8
    sub = lax.broadcasted_iota(jnp.int32, (8, TILE), 0)
    scale = [jnp.zeros((8, TILE), jnp.float32) for _ in range(parts)]
    cols = {}
    for j in range(BLOCK):
        top, at = divmod(j, 8)
        group = range(j + 1, (j // SUB + 1) * SUB)
        if j % SUB == 0:
            cols = {
                k: [
                    jnp.broadcast_to(v[h][:, base + k : base + k + 1], (8, TILE))
                    if h >= top
                    else None
                    for h in range(parts)
                ]
                for k in range(j, j + SUB)
            }
        root = lax.rsqrt(over_rows(cols[j][top], at))
        inverse = root * root
        scale[top] = jnp.where(sub == at, root, scale[top])
        v_row = over_rows(v[top], at)
        w_row = over_rows(w[top], at)
        c_row = {k: over_rows(cols[k][top], at) for k in group}
        for h in range(top, parts):
            if h == top and at == 7:
                continue
            factor = cols[j][h] * inverse
            if h == top:
                factor = jnp.where(sub > at, factor, 0.0)
            for k in group:
                cols[k][h] = cols[k][h] - factor * c_row[k]
            v[h] = v[h] - factor * v_row
            w[h] = w[h] - factor * w_row
    upper = jnp.concatenate([x * s for x, s in zip(v, scale)], axis=0)
    lower_inverse = jnp.concatenate([x * s for x, s in zip(w, scale)], axis=0)
    return upper, lower_inverse


def factor_tile(pivot, beside=()):
    beside = list(beside)
    row = lax.broadcasted_iota(jnp.int32, (TILE, TILE), 0)
    col = lax.broadcasted_iota(jnp.int32, (TILE, TILE), 1)
    rest = jnp.concatenate([pivot, (row == col).astype(jnp.float32)], axis=1)
    uppers, inverses = [], []
    blocks = TILE // BLOCK
    share = -(-len(beside) // blocks)
    for base in range(0, TILE, BLOCK):
        for _ in range(min(share, len(beside))):
            beside.pop(0)()
        v = [rest[at : at + 8, :TILE] for at in range(0, BLOCK, 8)]
        w = [rest[at : at + 8, TILE:] for at in range(0, BLOCK, 8)]
        upper, inverse = eliminate(v, w, base)
        uppers.append(upper)
        inverses.append(inverse)
        if base + BLOCK < TILE:
            update = mul_tn(upper, jnp.concatenate([upper, inverse], axis=1))
            rest = rest[BLOCK:] - update[base + BLOCK :]
    upper = jnp.where(row <= col, jnp.concatenate(uppers, axis=0), 0.0)
    inverse = jnp.where(row >= col, jnp.concatenate(inverses, axis=0), 0.0)
    return upper, inverse


def span(at):
    return slice(at * TILE, (at + 1) * TILE)


def advance(work, diagonal, k, beside=()):
    upper, inverse = factor_tile(work[span(k), span(k)], beside)
    diagonal[k] = upper.T
    work[span(k), span(PANELS + k)] = inverse
    at = min(k + 1, PANELS) * TILE
    wide = slice(at, at + (PANELS - 1) * TILE)
    work[span(k), wide] = mul_nn(inverse, work[span(k), wide])
    for i in range(k + 1, PANELS):
        old = slice(i * TILE, LEAD + k * TILE)
        both = mul_tn(work[span(k), span(i)], work[span(k), i * TILE : LEAD + (k + 1) * TILE])
        width = LEAD + k * TILE - i * TILE
        work[span(i), old] = work[span(i), old] - both[:, :width]
        work[span(i), span(PANELS + k)] = -both[:, width:]


def keep_inverse(work, inverse_ref, k):
    done = (k + 1) * TILE
    inverse_ref[span(k), :done] = work[span(k), LEAD : LEAD + done]
    if done < LEAD:
        inverse_ref[span(k), done:] = jnp.zeros((TILE, LEAD - done), jnp.float32)


def head_kernel(place, mine, other, inverse_ref, diagonal_ref, rest_ref, work):
    half = place[1] % 2
    chip = place[1] // 2

    def stored(column, slot):
        away = lax.rem(chip + 4 - column // 2, 4)
        here = mine[away, slot]
        there = other[away, slot]
        return jnp.where(half == column % 2, here, there)

    for k in range(PANELS):
        for i in range(k, PANELS):
            apart = i - k
            if apart < SLOTS:
                tile = stored(i, apart)
            else:
                tile = stored(k, PANELS - apart).T
            work[span(k), span(i)] = tile
    for k in range(HEAD):
        advance(work, diagonal_ref, k)
        keep_inverse(work, inverse_ref, k)
    rest_ref[...] = work[HEAD * TILE :, HEAD * TILE : LEAD + HEAD * TILE]


def tail_kernel(
    place, rest, head_inverse, head_diagonal, m0, m1, m2, m3, o0, o1, o2, o3,
    inverse_ref, diagonal_ref, high, low, own_column, work, panel, full,
):
    column = place[1]
    half = column % 2
    chip = column // 2
    for k in range(PANELS):
        away = lax.rem(chip + 4 - k // 2, 4)
        for at, (mine, other) in enumerate(((m0, o0), (m1, o1), (m2, o2), (m3, o3))):

            @pl.when((away == at) & (half == k % 2))
            def _():
                panel[:, k * TILE : (k + 1) * TILE] = mine[...].reshape(8 * TILE, TILE)

            @pl.when((away == at) & (half != k % 2))
            def _():
                panel[:, k * TILE : (k + 1) * TILE] = other[...].reshape(8 * TILE, TILE)

    work[HEAD * TILE :, HEAD * TILE : LEAD + HEAD * TILE] = rest[...]
    inverse_ref[: HEAD * TILE] = head_inverse[...]
    diagonal_ref[:HEAD] = head_diagonal[...]

    def product(rows, at, end):
        part = mul_nt(panel[rows, :end], inverse_ref[at:end, :end])
        high[rows, at:end], low[rows, at:end] = split(part)
        full[rows, at:end] = part

    quarters = [slice(at, at + 2 * TILE) for at in range(0, 8 * TILE, 2 * TILE)]
    for k in range(HEAD, PANELS):
        start, stop = CUTS[k - HEAD]
        beside = [functools.partial(product, rows, start, stop) for rows in quarters]
        advance(work, diagonal_ref, k, beside)
        keep_inverse(work, inverse_ref, k)
    product(slice(0, 8 * TILE), *CUTS[-1])
    wanted = jnp.minimum(column, PANELS - 1)
    for k in range(PANELS):

        @pl.when(wanted == k)
        def _():
            own_column[...] = full[:, k * TILE : (k + 1) * TILE].reshape(8, TILE, TILE)


def pick_kernel(place, *refs):
    *found, out = refs
    for slot in range(SLOTS):
        wanted = lax.rem(place[1] + 2 * PANELS - slot, PANELS)
        away = lax.rem(place[0] + 8 - wanted, 8)
        for at, ref in enumerate(found):

            @pl.when(away == at)
            def _():
                out[slot] = ref[...]


def tile_kernel(pos, front, own, given, out):
    out[...] = front[0, 0]
    for s, child in ((0, own), (1, given)):

        @pl.when((pos[s, 0, 0] == 0) & (pos[s, 1, 0] == 0))
        def _():
            out[...] += child[0, 0]


def row_kernel(pos, front, own, given, out):
    out[...] = front[0]
    for s, child in ((0, own), (1, given)):
        for m in range(8):
            u = pos[s, 1, m]

            @pl.when((pos[s, 0, 0] == 0) & (u >= 0))
            def _():
                out[m] += child[0, u]


def col_kernel(pos, front, own, top, below, out):
    out[...] = front[:, 0]
    for m in range(8):
        t = pos[0, 0, m]

        @pl.when((pos[0, 1, 0] == 0) & (t >= 0))
        def _():
            out[m] += own[t, 0]

        t2 = pos[1, 0, m]

        @pl.when((pos[1, 1, 0] == 0) & (t2 == 0))
        def _():
            out[m] += top[0, 0]

        @pl.when((pos[1, 1, 0] == 0) & (t2 > 0))
        def _():
            out[m] += below[t2 - 1]


def split(x):
    high = x.astype(jnp.bfloat16)
    low = (x - high.astype(jnp.float32)).astype(jnp.bfloat16)
    return high, low


def schur_kernel(
    pos, place, front, own, top, below, row_tiles, high, low, column_part, inverse, diagonal, out,
    panel, right,
):
    step = pl.program_id(0)
    row = place[0]
    column = place[1]
    for k in range(PANELS):
        for m in range(WIDTH):
            panel[k * TILE : (k + 1) * TILE, m * TILE : (m + 1) * TILE] = row_tiles[k, m]
    for at, end in CUTS:
        right[at:end, :] = mul_nn(inverse[at:end, :end], panel[:end, :])
    right_high, right_low = split(right[...])
    update = mul_nn(
        jnp.concatenate([low[...], high[...], high[...]], axis=1),
        jnp.concatenate([right_high, right_low, right_high], axis=0),
        None,
    )
    for l in range(8):
        for m in range(WIDTH):
            out[l, m] = front[l, m] - update[
                l * TILE : (l + 1) * TILE, m * TILE : (m + 1) * TILE
            ]
    for m in range(WIDTH):
        u = pos[0, 1, step * WIDTH + m]
        u2 = pos[1, 1, step * WIDTH + m]
        for l in range(8):
            t = pos[0, 0, l]
            t2 = pos[1, 0, l]

            @pl.when((t >= 0) & (u >= 0))
            def _():
                out[l, m] += own[t, u]

            @pl.when((t2 == 0) & (u2 >= 0))
            def _():
                out[l, m] += top[0, u2]

            @pl.when((t2 > 0) & (u2 >= 0))
            def _():
                out[l, m] += below[t2 - 1, u2]

    @pl.when((step == 0) & (column < PANELS))
    def _():
        for l in range(1, 8):
            out[l, 0] = column_part[l]

        @pl.when((row > column) | (row >= PANELS))
        def _():
            out[0, 0] = column_part[0]

        @pl.when(row == column)
        def _():
            out[0, 0] = diagonal[jnp.minimum(row, PANELS - 1)]

    pivot = jnp.minimum(row, PANELS - 1)
    for m in range(WIDTH):
        first = (step == 0) if m == 0 else False
        skip = jnp.logical_and(first, row >= column)

        @pl.when((row < PANELS) & jnp.logical_not(skip))
        def _():
            here = pl.ds(pl.multiple_of(pivot * TILE, TILE), TILE)
            out[0, m] = right[here, m * TILE : (m + 1) * TILE]


def whole(*shape):
    return pl.BlockSpec(shape, lambda *_: (0,) * len(shape))


def f32(*shape):
    return jax.ShapeDtypeStruct(shape, jnp.float32)


def places(lists, position, count):
    value = jnp.arange(count, dtype=jnp.int32) * 8 + position
    there = jnp.any(lists[:, None, :] == value[None, :, None], axis=2)
    same = (lists % 8 == position)[:, None, :]
    before = jnp.sum((lists[:, None, :] < value[None, :, None]) & same, axis=2, dtype=jnp.int32)
    return jnp.where(there, before, -1)


def sources(column):
    return [(column - slot) % PANELS for slot in range(SLOTS)]


def per_device(front, child_update, child_tiles):
    row_at = lax.axis_index("row")
    col_at = lax.axis_index("col")
    group_at = lax.axis_index("grp")
    local = front[0, 0, :, 0]
    own = child_update[0, 0, 0, :, 0]
    given = child_update[0, 1, 0, :, 0]
    both = ("row", "col")
    limit = pltpu.CompilerParams(vmem_limit_bytes=56 * 1024 * 1024)

    siblings = [(g, g ^ 1) for g in range(4)]
    top = lax.ppermute(given[:1], "grp", siblings)

    lists = jnp.stack([child_tiles[group_at, 0], child_tiles[jnp.bitwise_xor(group_at, 1), 1]])
    pos = jnp.stack([places(lists, row_at, 8), places(lists, col_at, 8)], axis=1)
    place = jnp.stack([row_at, col_at]).astype(jnp.int32)

    tile = pl.pallas_call(
        tile_kernel,
        grid=(1,),
        out_shape=f32(TILE, TILE),
        in_specs=[pl.BlockSpec(memory_space=SMEM)] + [whole(1, 1, TILE, TILE)] * 3,
        out_specs=whole(TILE, TILE),
        name="tile",
    )(pos, local, own, top)
    given, tile = lax.optimization_barrier((given, tile))
    left = lax.ppermute(given[1:, 0], "grp", siblings)
    below = lax.ppermute(given[1:], "grp", siblings)
    row_panel = pl.pallas_call(
        row_kernel,
        grid=(1,),
        out_shape=f32(8, TILE, TILE),
        in_specs=[
            pl.BlockSpec(memory_space=SMEM),
            whole(1, 8, TILE, TILE),
            whole(1, 5, TILE, TILE),
            whole(1, 5, TILE, TILE),
        ],
        out_specs=whole(8, TILE, TILE),
        name="row_panel",
    )(pos, local, own, top)

    found = [tile]
    for away in range(1, 8):
        step = [
            (z * 8 + c, (z + away) % 8 * 8 + c) for c in range(PANELS) for z in sources(c)
        ]
        found.append(lax.ppermute(tile, both, step))
    col_panel = pl.pallas_call(
        col_kernel,
        grid=(1,),
        out_shape=f32(8, TILE, TILE),
        in_specs=[
            pl.BlockSpec(memory_space=SMEM),
            whole(8, 1, TILE, TILE),
            whole(5, 1, TILE, TILE),
            whole(1, 1, TILE, TILE),
            whole(4, TILE, TILE),
        ],
        out_specs=whole(8, TILE, TILE),
        name="col_panel",
    )(pos, local, own, top, left)
    row_panel, col_panel, *found = lax.optimization_barrier((row_panel, col_panel, *found))
    row_tiles = lax.all_gather(row_panel, "row")
    picked = pl.pallas_call(
        pick_kernel,
        out_shape=f32(SLOTS, TILE, TILE),
        in_specs=[pl.BlockSpec(memory_space=SMEM)] + [pl.BlockSpec(memory_space=VMEM)] * 8,
        out_specs=pl.BlockSpec(memory_space=VMEM),
        name="pick",
    )(place, *found)
    across = [(c, c ^ 1) for c in range(8)]
    moved = [
        lax.ppermute(col_panel, "col", [(c, (c + away) % 8) for c in range(PANELS)])
        for away in (2, 4, 6)
    ]
    mine = [picked]
    for away in (2, 4, 6):
        mine.append(
            lax.ppermute(picked, "col", [(c, (c + away) % 8) for c in range(PANELS)])
        )
    mine = jnp.stack(mine)
    other = lax.ppermute(mine, "col", across)
    head_inverse, head_diagonal, rest = pl.pallas_call(
        head_kernel,
        out_shape=[
            f32(HEAD * TILE, LEAD), f32(HEAD, TILE, TILE), f32((PANELS - HEAD) * TILE, LEAD)
        ],
        in_specs=[pl.BlockSpec(memory_space=SMEM)] + [pl.BlockSpec(memory_space=VMEM)] * 2,
        out_specs=[pl.BlockSpec(memory_space=VMEM)] * 3,
        scratch_shapes=[pltpu.VMEM((LEAD, 2 * LEAD), jnp.float32)],
        compiler_params=limit,
        cost_estimate=pl.CostEstimate(
            flops=18_000_000_000, bytes_accessed=6_000_000, transcendentals=0
        ),
        name="head",
    )(place, mine, other)

    *moved, below, head_inverse = lax.optimization_barrier((*moved, below, head_inverse))
    col_mine = [col_panel, *moved]
    col_other = [lax.ppermute(part, "col", across) for part in col_mine]
    inverse, diagonal, high, low, column_part = pl.pallas_call(
        tail_kernel,
        out_shape=[
            f32(LEAD, LEAD),
            f32(PANELS, TILE, TILE),
            jax.ShapeDtypeStruct((8 * TILE, LEAD), jnp.bfloat16),
            jax.ShapeDtypeStruct((8 * TILE, LEAD), jnp.bfloat16),
            f32(8, TILE, TILE),
        ],
        in_specs=[pl.BlockSpec(memory_space=SMEM)] + [pl.BlockSpec(memory_space=VMEM)] * 11,
        out_specs=[pl.BlockSpec(memory_space=VMEM)] * 5,
        scratch_shapes=[
            pltpu.VMEM((LEAD, 2 * LEAD), jnp.float32),
            pltpu.VMEM((8 * TILE, LEAD), jnp.float32),
            pltpu.VMEM((8 * TILE, LEAD), jnp.float32),
        ],
        compiler_params=limit,
        cost_estimate=pl.CostEstimate(
            flops=15_000_000_000, bytes_accessed=6_000_000, transcendentals=0
        ),
        name="tail",
    )(place, rest, head_inverse, head_diagonal, *col_mine, *col_other)

    result = pl.pallas_call(
        schur_kernel,
        grid=(8 // WIDTH,),
        out_shape=f32(8, 8, TILE, TILE),
        in_specs=[
            pl.BlockSpec(memory_space=SMEM),
            pl.BlockSpec(memory_space=SMEM),
            pl.BlockSpec((8, WIDTH, TILE, TILE), lambda i: (0, i, 0, 0)),
            whole(5, 5, TILE, TILE),
            whole(1, 5, TILE, TILE),
            whole(4, 5, TILE, TILE),
            pl.BlockSpec((PANELS, WIDTH, TILE, TILE), lambda i: (0, i, 0, 0)),
            whole(8 * TILE, LEAD),
            whole(8 * TILE, LEAD),
            whole(8, TILE, TILE),
            whole(LEAD, LEAD),
            whole(PANELS, TILE, TILE),
        ],
        out_specs=pl.BlockSpec((8, WIDTH, TILE, TILE), lambda i: (0, i, 0, 0)),
        scratch_shapes=[
            pltpu.VMEM((LEAD, WIDTH * TILE), jnp.float32),
            pltpu.VMEM((LEAD, WIDTH * TILE), jnp.float32),
        ],
        compiler_params=limit,
        name="schur",
    )(
        pos, place, local, own, top, below, row_tiles, high, low, column_part, inverse, diagonal
    )
    return result[None, None, :, None]


def solution(mesh):
    in_specs = (
        P("grp", "row", None, "col", None, None, None),
        P("grp", None, "row", None, "col", None, None, None),
        P(),
    )
    out_specs = P("grp", "row", None, "col", None, None, None)
    return jax.shard_map(
        per_device, mesh=mesh, in_specs=in_specs, out_specs=out_specs, check_vma=False
    )
```

profile of v0, /device:TPU:1, one launch (start us, length us, event | category | flops | bytes accessed | tf_op | source)
XLA Modules:
  0.0 139.9 jit_solution(1944129978969275432)
XLA Ops:
  6.5 1.0 slice_bitcast_fusion.2
  7.5 2.2 %collective-permute-start = (f32[1,5,128,128]{3,2,1,0:T(8,128)S(1)}, f32[1,5,128,128]{3,2,1,0:T(8,128)S(1)}, u32[]{:S(2)}, u32[]{:S(2)}) collective-permute-start(f32[1,5,128,128]{3,2,1,0:T(8,128)S(1)} %slice_bitcast_fusion.2), channel_id=1, source_target_pairs={{0,64},{64,0},{128,192},{192,128},{1,65},{65,1},{129,193},{193,129... | collective-permute-start | bytes 983048 | tf_op jit(solution)/shard_map/ppermute | solution.py:357
  11.6 3.4 %slice_bitcast_fusion = (f32[5,5,128,128]{3,2,1,0:T(8,128)S(1)}, f32[5,5,128,128]{3,2,1,0:T(8,128)}) fusion(f32[1,2,1,5,1,5,128,128]{7,6,5,3,4,2,1,0:T(8,128)} %bitcast.35), kind=kLoop, calls=%fused_computation | loop fusion | bytes 6553600 | tf_op jit(solution)/shard_map/squeeze | solution.py:352
  16.7 1.6 %tile.1.refs_0_ = f32[128,128]{1,0:T(8,128)} custom-call(s32[2,2,8]{2,1,0:T(2,128)} %pad_add_fusion.pos, f32[8,8,128,128]{3,2,1,0:T(8,128)} %bitcast.30, f32[5,5,128,128]{3,2,1,0:T(8,128)} %get-tuple-element.62.own, f32[1,5,128,128]{3,2,1,0:T(8,128)} %copy-done), custom_call_target="tpu_custom_call" | custom-call | tf_op jit(solution)/shard_map/tile/pallas_call | solution.py:363
  18.3 2.3 %collective-permute-start.1 = (f32[4,128,128]{2,1,0:T(8,128)S(1)}, f32[4,128,128]{2,1,0:T(8,128)S(1)}, u32[]{:S(2)}, u32[]{:S(2)}) collective-permute-start(f32[4,128,128]{2,1,0:T(8,128)S(1)} %slice_bitcast_fusion.3), channel_id=1, source_target_pairs={{0,64},{64,0},{128,192},{192,128},{1,65},{65,1},{129,193},{193,129... | collective-permute-start | bytes 786440 | tf_op jit(solution)/shard_map/ppermute | solution.py:372
  20.6 3.7 %collective-permute-start.2 = (f32[128,128]{1,0:T(8,128)}, f32[128,128]{1,0:T(8,128)S(1)}, u32[]{:S(2)}, u32[]{:S(2)}) collective-permute-start(f32[128,128]{1,0:T(8,128)} %tile.1.refs_0_), channel_id=1, source_target_pairs={{0,8},{32,40},{24,32},{9,17},{1,9},{33,41},{18,26},{10,18},{2,10},... | collective-permute-start | bytes 196616 | tf_op jit(solution)/shard_map/ppermute | solution.py:393
  24.3 2.6 %collective-permute-start.3 = (f32[128,128]{1,0:T(8,128)}, f32[128,128]{1,0:T(8,128)S(1)}, u32[]{:S(2)}, u32[]{:S(2)}) collective-permute-start(f32[128,128]{1,0:T(8,128)} %tile.1.refs_0_), channel_id=1, source_target_pairs={{0,16},{32,48},{24,40},{9,25},{1,17},{33,49},{18,34},{10,26},{2,18... | collective-permute-start | bytes 196616 | tf_op jit(solution)/shard_map/ppermute | solution.py:393
  26.9 2.0 %collective-permute-start.4 = (f32[128,128]{1,0:T(8,128)}, f32[128,128]{1,0:T(8,128)S(1)}, u32[]{:S(2)}, u32[]{:S(2)}) collective-permute-start(f32[128,128]{1,0:T(8,128)} %tile.1.refs_0_), channel_id=1, source_target_pairs={{0,24},{32,56},{24,48},{9,33},{1,25},{33,57},{18,42},{10,34},{2,26... | collective-permute-start | bytes 196616 | tf_op jit(solution)/shard_map/ppermute | solution.py:393
  29.0 6.5 %collective-permute-start.5 = (f32[128,128]{1,0:T(8,128)}, f32[128,128]{1,0:T(8,128)S(1)}, u32[]{:S(2)}, u32[]{:S(2)}) collective-permute-start(f32[128,128]{1,0:T(8,128)} %tile.1.refs_0_), channel_id=1, source_target_pairs={{0,32},{32,0},{24,56},{9,41},{1,33},{33,1},{18,50},{10,42},{2,34},... | collective-permute-start | bytes 196616 | tf_op jit(solution)/shard_map/ppermute | solution.py:393
  35.5 1.3 collective-permute-start.6
  36.8 1.3 collective-permute-start.7
  38.1 1.9 %collective-permute-start.8 = (f32[128,128]{1,0:T(8,128)}, f32[128,128]{1,0:T(8,128)S(1)}, u32[]{:S(2)}, u32[]{:S(2)}) collective-permute-start(f32[128,128]{1,0:T(8,128)} %tile.1.refs_0_), channel_id=1, source_target_pairs={{0,56},{32,24},{24,16},{9,1},{1,57},{33,25},{18,10},{10,2},{2,58},... | collective-permute-start | bytes 196616 | tf_op jit(solution)/shard_map/ppermute | solution.py:393
  40.0 2.3 %row_panel.1 = f32[8,128,128]{2,1,0:T(8,128)} custom-call(s32[2,2,8]{2,1,0:T(2,128)} %pad_add_fusion.pos, f32[8,8,128,128]{3,2,1,0:T(8,128)} %bitcast.31, f32[5,5,128,128]{3,2,1,0:T(8,128)} %get-tuple-element.62.own, f32[1,5,128,128]{3,2,1,0:T(8,128)} %copy-done), custom_call_target="tpu_custom_call" | custom-call | tf_op jit(solution)/shard_map/row_panel/pallas_call | solution.py:374
  42.3 2.3 %col_panel.1.m0 = f32[8,128,128]{2,1,0:T(8,128)} custom-call(s32[2,2,8]{2,1,0:T(2,128)} %pad_add_fusion.pos, f32[8,8,128,128]{3,2,1,0:T(8,128)} %bitcast.32, f32[5,5,128,128]{3,2,1,0:T(8,128)} %get-tuple-element.62.own, f32[1,5,128,128]{3,2,1,0:T(8,128)} %copy-done, f32[4,128,128]{2,1,0:T(8,128)} %copy-done.4), custom_call_target="tpu_custom_call" | custom-call | tf_op jit(solution)/shard_map/col_panel/pallas_call | solution.py:394
  45.3 1.9 %pick.1 = f32[3,128,128]{2,1,0:T(8,128)} custom-call(s32[2]{0:T(128)} %pad_add_fusion.2.place, f32[128,128]{1,0:T(8,128)} %tile.1.refs_0_, f32[128,128]{1,0:T(8,128)} %copy-done.5, f32[128,128]{1,0:T(8,128)} %copy-done.6, f32[128,128]{1,0:T(8,128)} %copy-done.7, f32[128,128]{1,0:T(8,128)} %copy-done.8, f32[128,128]{1,0:T(8,128)} %copy-done.9, ...), custom_call_target="tpu_custom_call" | custom-call | tf_op jit(solution)/shard_map/pick/pallas_call | solution.py:410
  47.2 4.0 %collective-permute-start.13 = (f32[3,128,128]{2,1,0:T(8,128)}, f32[3,128,128]{2,1,0:T(8,128)S(1)}, u32[]{:S(2)}, u32[]{:S(2)}) collective-permute-start(f32[3,128,128]{2,1,0:T(8,128)} %pick.1), channel_id=1, source_target_pairs={{0,2},{1,3},{2,4},{3,5},{4,6},{8,10},{9,11},{10,12},{11,13},{12,14... | collective-permute-start | bytes 589832 | tf_op jit(solution)/shard_map/ppermute | solution.py:425
  51.3 1.3 collective-permute-start.14
  52.6 1.9 %collective-permute-start.15 = (f32[3,128,128]{2,1,0:T(8,128)}, f32[3,128,128]{2,1,0:T(8,128)S(1)}, u32[]{:S(2)}, u32[]{:S(2)}) collective-permute-start(f32[3,128,128]{2,1,0:T(8,128)} %pick.1), channel_id=1, source_target_pairs={{0,6},{1,7},{2,0},{3,1},{4,2},{8,14},{9,15},{10,8},{11,9},{12,10},... | collective-permute-start | bytes 589832 | tf_op jit(solution)/shard_map/ppermute | solution.py:425
  55.4 4.2 %collective-permute-done.14 = f32[3,128,128]{2,1,0:T(8,128)S(1)} collective-permute-done((f32[3,128,128]{2,1,0:T(8,128)}, f32[3,128,128]{2,1,0:T(8,128)S(1)}, u32[]{:S(2)}, u32[]{:S(2)}) %collective-permute-start.14) | collective-permute-done | bytes 196640 | tf_op jit(solution)/shard_map/ppermute | solution.py:425
  59.6 1.9 %collective-permute-done.15 = f32[3,128,128]{2,1,0:T(8,128)S(1)} collective-permute-done((f32[3,128,128]{2,1,0:T(8,128)}, f32[3,128,128]{2,1,0:T(8,128)S(1)}, u32[]{:S(2)}, u32[]{:S(2)}) %collective-permute-start.15) | collective-permute-done | bytes 196640 | tf_op jit(solution)/shard_map/ppermute | solution.py:425
  61.5 1.0 pad_maximum_fusion.mine
  62.5 1.4 %collective-permute-start.16 = (f32[4,3,128,128]{3,2,1,0:T(8,128)S(1)}, f32[4,3,128,128]{3,2,1,0:T(8,128)S(1)}, u32[]{:S(2)}, u32[]{:S(2)}) collective-permute-start(f32[4,3,128,128]{3,2,1,0:T(8,128)S(1)} %pad_maximum_fusion.mine), channel_id=1, source_target_pairs={{0,1},{1,0},{2,3},{3,2},{4,5},{5,4},{6,7},{7,6},{8,9},{9,8},{10,11... | collective-permute-start | bytes 2359304 | tf_op jit(solution)/shard_map/ppermute | solution.py:428
  64.3 3.6 %collective-permute-start.10 = (f32[8,128,128]{2,1,0:T(8,128)S(1)}, f32[8,128,128]{2,1,0:T(8,128)S(1)}, u32[]{:S(2)}, u32[]{:S(2)}) collective-permute-start(f32[8,128,128]{2,1,0:T(8,128)S(1)} %copy-done.3), channel_id=1, source_target_pairs={{0,4},{1,5},{2,6},{3,7},{4,0},{8,12},{9,13},{10,14},{11,15},{12,8}... | collective-permute-start | bytes 1572872 | tf_op jit(solution)/shard_map/ppermute | solution.py:419
  67.9 2.4 %collective-permute-start.11 = (f32[8,128,128]{2,1,0:T(8,128)S(1)}, f32[8,128,128]{2,1,0:T(8,128)S(1)}, u32[]{:S(2)}, u32[]{:S(2)}) collective-permute-start(f32[8,128,128]{2,1,0:T(8,128)S(1)} %copy-done.3), channel_id=1, source_target_pairs={{0,6},{1,7},{2,0},{3,1},{4,2},{8,14},{9,15},{10,8},{11,9},{12,10},... | collective-permute-start | bytes 1572872 | tf_op jit(solution)/shard_map/ppermute | solution.py:419
  70.3 3.0 %collective-permute-start.9 = (f32[8,128,128]{2,1,0:T(8,128)S(1)}, f32[8,128,128]{2,1,0:T(8,128)S(1)}, u32[]{:S(2)}, u32[]{:S(2)}) collective-permute-start(f32[8,128,128]{2,1,0:T(8,128)S(1)} %copy-done.3), channel_id=1, source_target_pairs={{0,2},{1,3},{2,4},{3,5},{4,6},{8,10},{9,11},{10,12},{11,13},{12,14... | collective-permute-start | bytes 1572872 | tf_op jit(solution)/shard_map/ppermute | solution.py:419
  73.2 1.9 %collective-permute-start.17 = (f32[8,128,128]{2,1,0:T(8,128)S(1)}, f32[8,128,128]{2,1,0:T(8,128)S(1)}, u32[]{:S(2)}, u32[]{:S(2)}) collective-permute-start(f32[8,128,128]{2,1,0:T(8,128)S(1)} %copy-done.3), channel_id=1, source_target_pairs={{0,1},{1,0},{2,3},{3,2},{4,5},{5,4},{6,7},{7,6},{8,9},{9,8},{10,11... | collective-permute-start | bytes 1572872 | tf_op jit(solution)/shard_map/ppermute | solution.py:446
  75.2 16.0 %head.1 = (f32[384,640]{1,0:T(8,128)}, f32[3,128,128]{2,1,0:T(8,128)}, f32[256,640]{1,0:T(8,128)}) custom-call(s32[2]{0:T(128)} %pad_add_fusion.2.place, f32[4,3,128,128]{3,2,1,0:T(8,128)} %copy-done.2, f32[4,3,128,128]{3,2,1,0:T(8,128)} %copy-done.12), custom_call_target="tpu_custom_call" | custom-call | flops 17999998976 | bytes 6000000 | tf_op jit(solution)/shard_map/head/pallas_call | solution.py:429
  91.2 1.3 collective-permute-done.11.m3
  92.4 2.2 %collective-permute-done.12.below = f32[4,5,128,128]{3,2,1,0:T(8,128)S(1)} collective-permute-done((f32[4,5,128,128]{3,2,1,0:T(8,128)S(1)}, f32[4,5,128,128]{3,2,1,0:T(8,128)S(1)}, u32[]{:S(2)}, u32[]{:S(2)}) %collective-permute-start.12) | collective-permute-done | bytes 1310752 | tf_op jit(solution)/shard_map/ppermute | solution.py:373
  95.8 1.0 collective-permute-done.18.o1
  99.1 17.2 %tail.1 = (f32[640,640]{1,0:T(8,128)}, f32[5,128,128]{2,1,0:T(8,128)}, bf16[1024,640]{1,0:T(8,128)(2,1)}, bf16[1024,640]{1,0:T(8,128)(2,1)}, f32[8,128,128]{2,1,0:T(8,128)}) custom-call(s32[2]{0:T(128)} %pad_add_fusion.2.place, f32[256,640]{1,0:T(8,128)} %get-tuple-element.44.rest, f32[384,640]{1,0:T(8,128)} %get-tuple-element.45.head_inverse, ...), custom_call_target="tpu_custom_call" | custom-call | flops 15000000512 | bytes 6000000 | tf_op jit(solution)/shard_map/tail/pallas_call | solution.py:447
  116.3 16.7 %schur.1 = f32[8,8,128,128]{3,2,1,0:T(8,128)} custom-call(s32[2,2,8]{2,1,0:T(2,128)} %pad_add_fusion.pos, s32[2]{0:T(128)} %pad_add_fusion.2.place, f32[8,8,128,128]{3,2,1,0:T(8,128)} %bitcast.33, f32[5,5,128,128]{3,2,1,0:T(8,128)} %get-tuple-element.62.own, f32[1,5,128,128]{3,2,1,0:T(8,128)} %copy-done, f32[4,5,128,128]{3,2,1,0:T(8,128)} %copy-done.1, ...), custom_call_target="tpu_custom_call" | custom-call | tf_op jit(solution)/shard_map/schur/pallas_call | solution.py:470
  (76 shorter events, 8.9 us)
Async XLA Ops:
  6.5 109.8 %all-gather.3.cloned.1.call-start = ((), (), s32[]{:S(2)}) async-start(), calls=%async_computation | async-start | bytes 4718592 | tf_op jit(solution)/shard_map/all_gather | solution.py:409
  7.5 8.4 %collective-permute-start = (f32[1,5,128,128]{3,2,1,0:T(8,128)S(1)}, f32[1,5,128,128]{3,2,1,0:T(8,128)S(1)}, u32[]{:S(2)}, u32[]{:S(2)}) collective-permute-start(f32[1,5,128,128]{3,2,1,0:T(8,128)S(1)} %slice_bitcast_fusion.2), channel_id=1, source_target_pairs={{0,64},{64,0},{128,192},{192,128},{1,65},{65,1},{129,193},{193,129... | collective-permute-start | bytes 983048 | tf_op jit(solution)/shard_map/ppermute | solution.py:357
  18.3 19.8 %collective-permute-start.1 = (f32[4,128,128]{2,1,0:T(8,128)S(1)}, f32[4,128,128]{2,1,0:T(8,128)S(1)}, u32[]{:S(2)}, u32[]{:S(2)}) collective-permute-start(f32[4,128,128]{2,1,0:T(8,128)S(1)} %slice_bitcast_fusion.3), channel_id=1, source_target_pairs={{0,64},{64,0},{128,192},{192,128},{1,65},{65,1},{129,193},{193,129... | collective-permute-start | bytes 786440 | tf_op jit(solution)/shard_map/ppermute | solution.py:372
  20.6 14.9 %collective-permute-start.2 = (f32[128,128]{1,0:T(8,128)}, f32[128,128]{1,0:T(8,128)S(1)}, u32[]{:S(2)}, u32[]{:S(2)}) collective-permute-start(f32[128,128]{1,0:T(8,128)} %tile.1.refs_0_), channel_id=1, source_target_pairs={{0,8},{32,40},{24,32},{9,17},{1,9},{33,41},{18,26},{10,18},{2,10},... | collective-permute-start | bytes 196616 | tf_op jit(solution)/shard_map/ppermute | solution.py:393
  24.3 12.5 %collective-permute-start.3 = (f32[128,128]{1,0:T(8,128)}, f32[128,128]{1,0:T(8,128)S(1)}, u32[]{:S(2)}, u32[]{:S(2)}) collective-permute-start(f32[128,128]{1,0:T(8,128)} %tile.1.refs_0_), channel_id=1, source_target_pairs={{0,16},{32,48},{24,40},{9,25},{1,17},{33,49},{18,34},{10,26},{2,18... | collective-permute-start | bytes 196616 | tf_op jit(solution)/shard_map/ppermute | solution.py:393
  26.9 17.7 %collective-permute-start.4 = (f32[128,128]{1,0:T(8,128)}, f32[128,128]{1,0:T(8,128)S(1)}, u32[]{:S(2)}, u32[]{:S(2)}) collective-permute-start(f32[128,128]{1,0:T(8,128)} %tile.1.refs_0_), channel_id=1, source_target_pairs={{0,24},{32,56},{24,48},{9,33},{1,25},{33,57},{18,42},{10,34},{2,26... | collective-permute-start | bytes 196616 | tf_op jit(solution)/shard_map/ppermute | solution.py:393
  29.0 15.6 %collective-permute-start.5 = (f32[128,128]{1,0:T(8,128)}, f32[128,128]{1,0:T(8,128)S(1)}, u32[]{:S(2)}, u32[]{:S(2)}) collective-permute-start(f32[128,128]{1,0:T(8,128)} %tile.1.refs_0_), channel_id=1, source_target_pairs={{0,32},{32,0},{24,56},{9,41},{1,33},{33,1},{18,50},{10,42},{2,34},... | collective-permute-start | bytes 196616 | tf_op jit(solution)/shard_map/ppermute | solution.py:393
  35.4 6.8 %copy-start.5 = (f32[128,128]{1,0:T(8,128)}, f32[128,128]{1,0:T(8,128)S(1)}, u32[]{:S(2)}) copy-start(f32[128,128]{1,0:T(8,128)S(1)} %collective-permute-done.2.refs_1_) | copy-start | bytes 196612
  35.5 9.2 %collective-permute-start.6 = (f32[128,128]{1,0:T(8,128)}, f32[128,128]{1,0:T(8,128)S(1)}, u32[]{:S(2)}, u32[]{:S(2)}) collective-permute-start(f32[128,128]{1,0:T(8,128)} %tile.1.refs_0_), channel_id=1, source_target_pairs={{0,40},{32,8},{24,0},{9,49},{1,41},{33,9},{18,58},{10,50},{2,42},{... | collective-permute-start | bytes 196616 | tf_op jit(solution)/shard_map/ppermute | solution.py:393
  36.8 5.5 %copy-start.6 = (f32[128,128]{1,0:T(8,128)}, f32[128,128]{1,0:T(8,128)S(1)}, u32[]{:S(2)}) copy-start(f32[128,128]{1,0:T(8,128)S(1)} %collective-permute-done.3.refs_2_) | copy-start | bytes 196612
  36.8 7.9 %collective-permute-start.7 = (f32[128,128]{1,0:T(8,128)}, f32[128,128]{1,0:T(8,128)S(1)}, u32[]{:S(2)}, u32[]{:S(2)}) collective-permute-start(f32[128,128]{1,0:T(8,128)} %tile.1.refs_0_), channel_id=1, source_target_pairs={{0,48},{32,16},{24,8},{9,57},{1,49},{33,17},{18,2},{10,58},{2,50},... | collective-permute-start | bytes 196616 | tf_op jit(solution)/shard_map/ppermute | solution.py:393
  38.1 4.2 %copy-start.4 = (f32[4,128,128]{2,1,0:T(8,128)}, f32[4,128,128]{2,1,0:T(8,128)S(1)}, u32[]{:S(2)}) copy-start(f32[4,128,128]{2,1,0:T(8,128)S(1)} %collective-permute-done.1.below) | copy-start | bytes 786436
  38.1 6.6 %collective-permute-start.8 = (f32[128,128]{1,0:T(8,128)}, f32[128,128]{1,0:T(8,128)S(1)}, u32[]{:S(2)}, u32[]{:S(2)}) collective-permute-start(f32[128,128]{1,0:T(8,128)} %tile.1.refs_0_), channel_id=1, source_target_pairs={{0,56},{32,24},{24,16},{9,1},{1,57},{33,25},{18,10},{10,2},{2,58},... | collective-permute-start | bytes 196616 | tf_op jit(solution)/shard_map/ppermute | solution.py:393
  47.2 8.1 %collective-permute-start.13 = (f32[3,128,128]{2,1,0:T(8,128)}, f32[3,128,128]{2,1,0:T(8,128)S(1)}, u32[]{:S(2)}, u32[]{:S(2)}) collective-permute-start(f32[3,128,128]{2,1,0:T(8,128)} %pick.1), channel_id=1, source_target_pairs={{0,2},{1,3},{2,4},{3,5},{4,6},{8,10},{9,11},{10,12},{11,13},{12,14... | collective-permute-start | bytes 589832 | tf_op jit(solution)/shard_map/ppermute | solution.py:425
  51.3 8.3 %collective-permute-start.14 = (f32[3,128,128]{2,1,0:T(8,128)}, f32[3,128,128]{2,1,0:T(8,128)S(1)}, u32[]{:S(2)}, u32[]{:S(2)}) collective-permute-start(f32[3,128,128]{2,1,0:T(8,128)} %pick.1), channel_id=1, source_target_pairs={{0,4},{1,5},{2,6},{3,7},{4,0},{8,12},{9,13},{10,14},{11,15},{12,8}... | collective-permute-start | bytes 589832 | tf_op jit(solution)/shard_map/ppermute | solution.py:425
  52.6 8.9 %collective-permute-start.15 = (f32[3,128,128]{2,1,0:T(8,128)}, f32[3,128,128]{2,1,0:T(8,128)S(1)}, u32[]{:S(2)}, u32[]{:S(2)}) collective-permute-start(f32[3,128,128]{2,1,0:T(8,128)} %pick.1), channel_id=1, source_target_pairs={{0,6},{1,7},{2,0},{3,1},{4,2},{8,14},{9,15},{10,8},{11,9},{12,10},... | collective-permute-start | bytes 589832 | tf_op jit(solution)/shard_map/ppermute | solution.py:425
  62.5 12.7 %copy-start.2 = (f32[4,3,128,128]{3,2,1,0:T(8,128)}, f32[4,3,128,128]{3,2,1,0:T(8,128)S(1)}, u32[]{:S(2)}) copy-start(f32[4,3,128,128]{3,2,1,0:T(8,128)S(1)} %pad_maximum_fusion.mine) | copy-start | bytes 2359300
  62.5 10.8 %collective-permute-start.16 = (f32[4,3,128,128]{3,2,1,0:T(8,128)S(1)}, f32[4,3,128,128]{3,2,1,0:T(8,128)S(1)}, u32[]{:S(2)}, u32[]{:S(2)}) collective-permute-start(f32[4,3,128,128]{3,2,1,0:T(8,128)S(1)} %pad_maximum_fusion.mine), channel_id=1, source_target_pairs={{0,1},{1,0},{2,3},{3,2},{4,5},{5,4},{6,7},{7,6},{8,9},{9,8},{10,11... | collective-permute-start | bytes 2359304 | tf_op jit(solution)/shard_map/ppermute | solution.py:428
  64.0 30.6 %collective-permute-start.12 = (f32[4,5,128,128]{3,2,1,0:T(8,128)S(1)}, f32[4,5,128,128]{3,2,1,0:T(8,128)S(1)}, u32[]{:S(2)}, u32[]{:S(2)}) collective-permute-start(f32[4,5,128,128]{3,2,1,0:T(8,128)S(1)} %slice.24), channel_id=1, source_target_pairs={{0,64},{64,0},{128,192},{192,128},{1,65},{65,1},{129,193},{193,129... | collective-permute-start | bytes 3932168 | tf_op jit(solution)/shard_map/ppermute | solution.py:373
  64.3 26.9 %collective-permute-start.10 = (f32[8,128,128]{2,1,0:T(8,128)S(1)}, f32[8,128,128]{2,1,0:T(8,128)S(1)}, u32[]{:S(2)}, u32[]{:S(2)}) collective-permute-start(f32[8,128,128]{2,1,0:T(8,128)S(1)} %copy-done.3), channel_id=1, source_target_pairs={{0,4},{1,5},{2,6},{3,7},{4,0},{8,12},{9,13},{10,14},{11,15},{12,8}... | collective-permute-start | bytes 1572872 | tf_op jit(solution)/shard_map/ppermute | solution.py:419
  67.9 24.6 %collective-permute-start.11 = (f32[8,128,128]{2,1,0:T(8,128)S(1)}, f32[8,128,128]{2,1,0:T(8,128)S(1)}, u32[]{:S(2)}, u32[]{:S(2)}) collective-permute-start(f32[8,128,128]{2,1,0:T(8,128)S(1)} %copy-done.3), channel_id=1, source_target_pairs={{0,6},{1,7},{2,0},{3,1},{4,2},{8,14},{9,15},{10,8},{11,9},{12,10},... | collective-permute-start | bytes 1572872 | tf_op jit(solution)/shard_map/ppermute | solution.py:419
  70.3 22.2 %collective-permute-start.9 = (f32[8,128,128]{2,1,0:T(8,128)S(1)}, f32[8,128,128]{2,1,0:T(8,128)S(1)}, u32[]{:S(2)}, u32[]{:S(2)}) collective-permute-start(f32[8,128,128]{2,1,0:T(8,128)S(1)} %copy-done.3), channel_id=1, source_target_pairs={{0,2},{1,3},{2,4},{3,5},{4,6},{8,10},{9,11},{10,12},{11,13},{12,14... | collective-permute-start | bytes 1572872 | tf_op jit(solution)/shard_map/ppermute | solution.py:419
  73.2 1.9 %copy-start.12 = (f32[4,3,128,128]{3,2,1,0:T(8,128)}, f32[4,3,128,128]{3,2,1,0:T(8,128)S(1)}, u32[]{:S(2)}) copy-start(f32[4,3,128,128]{3,2,1,0:T(8,128)S(1)} %collective-permute-done.16.other) | copy-start | bytes 2359300
  73.2 22.6 %collective-permute-start.17 = (f32[8,128,128]{2,1,0:T(8,128)S(1)}, f32[8,128,128]{2,1,0:T(8,128)S(1)}, u32[]{:S(2)}, u32[]{:S(2)}) collective-permute-start(f32[8,128,128]{2,1,0:T(8,128)S(1)} %copy-done.3), channel_id=1, source_target_pairs={{0,1},{1,0},{2,3},{3,2},{4,5},{5,4},{6,7},{7,6},{8,9},{9,8},{10,11... | collective-permute-start | bytes 1572872 | tf_op jit(solution)/shard_map/ppermute | solution.py:446
  91.2 7.2 %copy-start.13 = (f32[8,128,128]{2,1,0:T(8,128)}, f32[8,128,128]{2,1,0:T(8,128)S(1)}, u32[]{:S(2)}) copy-start(f32[8,128,128]{2,1,0:T(8,128)S(1)} %collective-permute-done.10.m2) | copy-start | bytes 1572868
  92.4 5.9 %copy-start.14 = (f32[8,128,128]{2,1,0:T(8,128)}, f32[8,128,128]{2,1,0:T(8,128)S(1)}, u32[]{:S(2)}) copy-start(f32[8,128,128]{2,1,0:T(8,128)S(1)} %collective-permute-done.11.m3) | copy-start | bytes 1572868
  92.4 5.9 %copy-start.15 = (f32[8,128,128]{2,1,0:T(8,128)}, f32[8,128,128]{2,1,0:T(8,128)S(1)}, u32[]{:S(2)}) copy-start(f32[8,128,128]{2,1,0:T(8,128)S(1)} %collective-permute-done.9.m1) | copy-start | bytes 1572868
  94.6 21.7 %copy-start.1 = (f32[4,5,128,128]{3,2,1,0:T(8,128)}, f32[4,5,128,128]{3,2,1,0:T(8,128)S(1)}, u32[]{:S(2)}) copy-start(f32[4,5,128,128]{3,2,1,0:T(8,128)S(1)} %collective-permute-done.12.below) | copy-start | bytes 3932164
  94.6 2.2 %collective-permute-start.18 = (f32[8,128,128]{2,1,0:T(8,128)S(1)}, f32[8,128,128]{2,1,0:T(8,128)S(1)}, u32[]{:S(2)}, u32[]{:S(2)}) collective-permute-start(f32[8,128,128]{2,1,0:T(8,128)S(1)} %collective-permute-done.9.m1), channel_id=1, source_target_pairs={{0,1},{1,0},{2,3},{3,2},{4,5},{5,4},{6,7},{7,6},{8,9},{9,8},{10,11... | collective-permute-start | bytes 1572872 | tf_op jit(solution)/shard_map/ppermute | solution.py:446
  95.3 2.3 %collective-permute-start.19 = (f32[8,128,128]{2,1,0:T(8,128)S(1)}, f32[8,128,128]{2,1,0:T(8,128)S(1)}, u32[]{:S(2)}, u32[]{:S(2)}) collective-permute-start(f32[8,128,128]{2,1,0:T(8,128)S(1)} %collective-permute-done.10.m2), channel_id=1, source_target_pairs={{0,1},{1,0},{2,3},{3,2},{4,5},{5,4},{6,7},{7,6},{8,9},{9,8},{10,11... | collective-permute-start | bytes 1572872 | tf_op jit(solution)/shard_map/ppermute | solution.py:446
  95.3 3.0 %collective-permute-start.20 = (f32[8,128,128]{2,1,0:T(8,128)S(1)}, f32[8,128,128]{2,1,0:T(8,128)S(1)}, u32[]{:S(2)}, u32[]{:S(2)}) collective-permute-start(f32[8,128,128]{2,1,0:T(8,128)S(1)} %collective-permute-done.11.m3), channel_id=1, source_target_pairs={{0,1},{1,0},{2,3},{3,2},{4,5},{5,4},{6,7},{7,6},{8,9},{9,8},{10,11... | collective-permute-start | bytes 1572872 | tf_op jit(solution)/shard_map/ppermute | solution.py:446
  95.8 2.5 %copy-start.16 = (f32[8,128,128]{2,1,0:T(8,128)}, f32[8,128,128]{2,1,0:T(8,128)S(1)}, u32[]{:S(2)}) copy-start(f32[8,128,128]{2,1,0:T(8,128)S(1)} %collective-permute-done.17.o0) | copy-start | bytes 1572868
  (10 other events, 9.0 us)
Sparse Core Ops, SparseCore 0:
  44.8 56.6 all-gather.2
where the time goes:
time: 141 us; the launch traced here: 140 us
  Pallas kernels  57.9 us (41%)
  starting transfers between devices  44.9 us (32%)
  waiting for transfers between devices  13.9 us (10%)
  between operations  13.7 us (10%)
  local copies, waits for them, and re-layouts  6.82 us (5%)
  other arithmetic  2.65 us (2%)
    ppermute x7, starting transfers between devices, per_device(): found.append(lax.ppermute(tile, both, step))  19.4 us
    pallas_call x1, Pallas kernels, per_device(): pl.pallas_call(tail_kernel, out_shape=[f32(LEAD, LEAD), f32(PANELS, TILE,...  17.2 us
    pallas_call x1, Pallas kernels, per_device(): pl.pallas_call(schur_kernel, grid=(8 // WIDTH,), out_shape=f32(8, 8, TILE...  16.7 us
    pallas_call x1, Pallas kernels, per_device(): pl.pallas_call(head_kernel, out_shape=[f32(HEAD * TILE, LEAD), f32(HEAD,...  16 us
    ppermute x3, starting transfers between devices, per_device(): lax.ppermute(col_panel, 'col', [(c, (c + away) % 8) for c in range(PANELS)])  8.93 us
    ppermute x3, starting transfers between devices, per_device(): lax.ppermute(picked, 'col', [(c, (c + away) % 8) for c in range(PANELS)])  7.25 us
    ppermute x3, waiting for transfers between devices, per_device(): lax.ppermute(picked, 'col', [(c, (c + away) % 8) for c in range(PANELS)])  6.97 us
    squeeze x1, local copies, waits for them, and re-layouts, per_device(): given = child_update[0, 1, 0, :, 0]  3.41 us
  transfers between devices with their start and end apart: 22, of which 9 were waited for; matrix products, arithmetic and copies ran while one was open for 5% of the time, Pallas kernels for 28%

commit v1 on v0

--- a/solution.py
+++ b/solution.py
@@ -14,6 +14,7 @@
 SUB = 16
 SLOTS = 3
 HEAD = 3
+LAST = HEAD + 1
 WIDTH = 2
 CUTS = ((0, 256), (256, 512), (512, 640))
 HIGHEST = lax.Precision.HIGHEST
@@ -110,9 +111,9 @@
     return slice(at * TILE, (at + 1) * TILE)
 
 
-def advance(work, diagonal, k, beside=()):
+def advance(work, diagonal, k, beside=(), first=0):
     upper, inverse = factor_tile(work[span(k), span(k)], beside)
-    diagonal[k] = upper.T
+    diagonal[k - first] = upper.T
     work[span(k), span(PANELS + k)] = inverse
     at = min(k + 1, PANELS) * TILE
     wide = slice(at, at + (PANELS - 1) * TILE)
@@ -156,8 +157,17 @@
     rest_ref[...] = work[HEAD * TILE :, HEAD * TILE : LEAD + HEAD * TILE]
 
 
+def middle_kernel(rest, inverse_ref, diagonal_ref, rest_ref, work):
+    work[HEAD * TILE :, HEAD * TILE : LEAD + HEAD * TILE] = rest[...]
+    advance(work, diagonal_ref, HEAD, first=HEAD)
+    inverse_ref[:, : LAST * TILE] = work[span(HEAD), LEAD : LEAD + LAST * TILE]
+    inverse_ref[:, LAST * TILE :] = jnp.zeros((TILE, TILE), jnp.float32)
+    rest_ref[...] = work[LAST * TILE :, LAST * TILE : LEAD + LAST * TILE]
+
+
 def tail_kernel(
-    place, rest, head_inverse, head_diagonal, m0, m1, m2, m3, o0, o1, o2, o3,
+    place, rest, head_inverse, head_diagonal, middle_inverse, middle_diagonal,
+    m0, m1, m2, m3, o0, o1, o2, o3,
     inverse_ref, diagonal_ref, high, low, own_column, work, panel, full,
 ):
     column = place[1]
@@ -175,9 +185,11 @@
             def _():
                 panel[:, k * TILE : (k + 1) * TILE] = other[...].reshape(8 * TILE, TILE)
 
-    work[HEAD * TILE :, HEAD * TILE : LEAD + HEAD * TILE] = rest[...]
+    work[LAST * TILE :, LAST * TILE : LEAD + LAST * TILE] = rest[...]
     inverse_ref[: HEAD * TILE] = head_inverse[...]
+    inverse_ref[HEAD * TILE : LAST * TILE] = middle_inverse[...]
     diagonal_ref[:HEAD] = head_diagonal[...]
+    diagonal_ref[HEAD] = middle_diagonal[0]
 
     def product(rows, at, end):
         part = mul_nt(panel[rows, :end], inverse_ref[at:end, :end])
@@ -185,11 +197,13 @@
         full[rows, at:end] = part
 
     quarters = [slice(at, at + 2 * TILE) for at in range(0, 8 * TILE, 2 * TILE)]
-    for k in range(HEAD, PANELS):
-        start, stop = CUTS[k - HEAD]
-        beside = [functools.partial(product, rows, start, stop) for rows in quarters]
-        advance(work, diagonal_ref, k, beside)
-        keep_inverse(work, inverse_ref, k)
+    beside = [
+        functools.partial(product, rows, start, stop)
+        for start, stop in CUTS[:-1]
+        for rows in quarters
+    ]
+    advance(work, diagonal_ref, LAST, beside)
+    keep_inverse(work, inverse_ref, LAST)
     product(slice(0, 8 * TILE), *CUTS[-1])
     wanted = jnp.minimum(column, PANELS - 1)
     for k in range(PANELS):
@@ -351,7 +365,8 @@
     own = child_update[0, 0, 0, :, 0]
     given = child_update[0, 1, 0, :, 0]
     both = ("row", "col")
-    limit = pltpu.CompilerParams(vmem_limit_bytes=56 * 1024 * 1024)
+    limit = pltpu.CompilerParams(vmem_limit_bytes=36 * 1024 * 1024)
+    most = pltpu.CompilerParams(vmem_limit_bytes=50 * 1024 * 1024)
 
     siblings = [(g, g ^ 1) for g in range(4)]
     top = lax.ppermute(given[:1], "grp", siblings)
@@ -391,6 +406,16 @@
             (z * 8 + c, (z + away) % 8 * 8 + c) for c in range(PANELS) for z in sources(c)
         ]
         found.append(lax.ppermute(tile, both, step))
+    row_panel, left, *found = lax.optimization_barrier((row_panel, left, *found))
+    row_tiles = lax.all_gather(row_panel, "row")
+    picked = pl.pallas_call(
+        pick_kernel,
+        out_shape=f32(SLOTS, TILE, TILE),
+        in_specs=[pl.BlockSpec(memory_space=SMEM)] + [pl.BlockSpec(memory_space=VMEM)] * 8,
+        out_specs=pl.BlockSpec(memory_space=VMEM),
+        name="pick",
+    )(place, *found)
+    across = [(c, c ^ 1) for c in range(8)]
     col_panel = pl.pallas_call(
         col_kernel,
         grid=(1,),
@@ -405,26 +430,17 @@
         out_specs=whole(8, TILE, TILE),
         name="col_panel",
     )(pos, local, own, top, left)
-    row_panel, col_panel, *found = lax.optimization_barrier((row_panel, col_panel, *found))
-    row_tiles = lax.all_gather(row_panel, "row")
-    picked = pl.pallas_call(
-        pick_kernel,
-        out_shape=f32(SLOTS, TILE, TILE),
-        in_specs=[pl.BlockSpec(memory_space=SMEM)] + [pl.BlockSpec(memory_space=VMEM)] * 8,
-        out_specs=pl.BlockSpec(memory_space=VMEM),
-        name="pick",
-    )(place, *found)
-    across = [(c, c ^ 1) for c in range(8)]
-    moved = [
-        lax.ppermute(col_panel, "col", [(c, (c + away) % 8) for c in range(PANELS)])
-        for away in (2, 4, 6)
-    ]
     mine = [picked]
     for away in (2, 4, 6):
         mine.append(
             lax.ppermute(picked, "col", [(c, (c + away) % 8) for c in range(PANELS)])
         )
+    *mine, col_panel = lax.optimization_barrier((*mine, col_panel))
     mine = jnp.stack(mine)
+    moved = [
+        lax.ppermute(col_panel, "col", [(c, (c + away) % 8) for c in range(PANELS)])
+        for away in (2, 4, 6)
+    ]
     other = lax.ppermute(mine, "col", across)
     head_inverse, head_diagonal, rest = pl.pallas_call(
         head_kernel,
@@ -441,9 +457,22 @@
         name="head",
     )(place, mine, other)
 
-    *moved, below, head_inverse = lax.optimization_barrier((*moved, below, head_inverse))
+    *moved, rest = lax.optimization_barrier((*moved, rest))
     col_mine = [col_panel, *moved]
     col_other = [lax.ppermute(part, "col", across) for part in col_mine]
+    middle_inverse, middle_diagonal, rest = pl.pallas_call(
+        middle_kernel,
+        out_shape=[f32(TILE, LEAD), f32(1, TILE, TILE), f32(TILE, LEAD)],
+        in_specs=[pl.BlockSpec(memory_space=VMEM)],
+        out_specs=[pl.BlockSpec(memory_space=VMEM)] * 3,
+        scratch_shapes=[pltpu.VMEM((LEAD, 2 * LEAD), jnp.float32)],
+        compiler_params=limit,
+        cost_estimate=pl.CostEstimate(
+            flops=6_000_000_000, bytes_accessed=2_000_000, transcendentals=0
+        ),
+        name="middle",
+    )(rest)
+    below, rest = lax.optimization_barrier((below, rest))
     inverse, diagonal, high, low, column_part = pl.pallas_call(
         tail_kernel,
         out_shape=[
@@ -453,7 +482,7 @@
             jax.ShapeDtypeStruct((8 * TILE, LEAD), jnp.bfloat16),
             f32(8, TILE, TILE),
         ],
-        in_specs=[pl.BlockSpec(memory_space=SMEM)] + [pl.BlockSpec(memory_space=VMEM)] * 11,
+        in_specs=[pl.BlockSpec(memory_space=SMEM)] + [pl.BlockSpec(memory_space=VMEM)] * 13,
         out_specs=[pl.BlockSpec(memory_space=VMEM)] * 5,
         scratch_shapes=[
             pltpu.VMEM((LEAD, 2 * LEAD), jnp.float32),
@@ -462,10 +491,10 @@
         ],
         compiler_params=limit,
         cost_estimate=pl.CostEstimate(
-            flops=15_000_000_000, bytes_accessed=6_000_000, transcendentals=0
+            flops=9_000_000_000, bytes_accessed=6_000_000, transcendentals=0
         ),
         name="tail",
-    )(place, rest, head_inverse, head_diagonal, *col_mine, *col_other)
+    )(place, rest, head_inverse, head_diagonal, middle_inverse, middle_diagonal, *col_mine, *col_other)
 
     result = pl.pallas_call(
         schur_kernel,
@@ -490,7 +519,7 @@
             pltpu.VMEM((LEAD, WIDTH * TILE), jnp.float32),
             pltpu.VMEM((LEAD, WIDTH * TILE), jnp.float32),
         ],
-        compiler_params=limit,
+        compiler_params=most,
         name="schur",
     )(
         pos, place, local, own, top, below, row_tiles, high, low, column_part, inverse, diagonal

time: 141 us -> 134 us (0.950)
  Pallas kernels: 57.9 us -> 50.6 us
  waiting for transfers between devices: 13.9 us -> 9.94 us
  local copies, waits for them, and re-layouts: 6.82 us -> 10 us
  starting transfers between devices: 44.9 us -> 47.1 us
    pallas_call x1, Pallas kernels: 17.2 us -> 8.17 us  [per_device(): pl.pallas_call(tail_kernel, out_shape=[f32(LEAD, LEAD), f32(PANELS, TILE,...]
    pallas_call x0 -> x1, Pallas kernels: none -> 4.44 us  [per_device(): pl.pallas_call(middle_kernel, out_shape=[f32(TILE, LEAD), f32(1, TILE, TI...]
    unnamed x40 -> x36, local copies, waits for them, and re-layouts: 1.62 us -> 4.79 us
    ppermute x4, starting transfers between devices: 3.12 us -> 5.99 us  [per_device(): col_other = [lax.ppermute(part, 'col', across) for part in col_mine]]
    ppermute x4, waiting for transfers between devices: 2.52 us -> 0.01 us  [per_device(): col_other = [lax.ppermute(part, 'col', across) for part in col_mine]]
    ppermute x3, waiting for transfers between devices: 6.97 us -> 4.64 us  [per_device(): lax.ppermute(picked, 'col', [(c, (c + away) % 8) for c in range(PANELS)])]
    ppermute x1, waiting for transfers between devices: 2.16 us -> 0.01 us  [per_device(): below = lax.ppermute(given[1:], 'grp', siblings)]
    ppermute x3, starting transfers between devices: 8.93 us -> 6.8 us  [per_device(): lax.ppermute(col_panel, 'col', [(c, (c + away) % 8) for c in range(PANELS)])]
  transfers between devices with their start and end apart: 22 -> 22, of which waited for: 9 -> 5; matrix products, arithmetic and copies ran while one was open for 5% -> 4% of each run, Pallas kernels for 28% -> 25%
where the time goes in v1:
time: 134 us; the launch traced here: 133 us
  Pallas kernels  50.6 us (38%)
  starting transfers between devices  47.1 us (35%)
  between operations  13.8 us (10%)
  local copies, waits for them, and re-layouts  10 us (7%)
  waiting for transfers between devices  9.94 us (7%)
  other arithmetic  1.69 us (1%)
    ppermute x7, starting transfers between devices, per_device(): found.append(lax.ppermute(tile, both, step))  19.4 us
    pallas_call x1, Pallas kernels, per_device(): pl.pallas_call(schur_kernel, grid=(8 // WIDTH,), out_shape=f32(8, 8, TILE...  15.7 us
    pallas_call x1, Pallas kernels, per_device(): pl.pallas_call(head_kernel, out_shape=[f32(HEAD * TILE, LEAD), f32(HEAD,...  14.3 us
    ppermute x3, starting transfers between devices, per_device(): lax.ppermute(picked, 'col', [(c, (c + away) % 8) for c in range(PANELS)])  8.76 us
    pallas_call x1, Pallas kernels, per_device(): pl.pallas_call(tail_kernel, out_shape=[f32(LEAD, LEAD), f32(PANELS, TILE,...  8.17 us
    ppermute x3, starting transfers between devices, per_device(): lax.ppermute(col_panel, 'col', [(c, (c + away) % 8) for c in range(PANELS)])  6.8 us
    ppermute x4, starting transfers between devices, per_device(): col_other = [lax.ppermute(part, 'col', across) for part in col_mine]  5.99 us
    unnamed x36, local copies, waits for them, and re-layouts  4.79 us
  transfers between devices with their start and end apart: 22, of which 5 were waited for; matrix products, arithmetic and copies ran while one was open for 4% of the time, Pallas kernels for 25%

profile of v1, /device:TPU:1, one launch (start us, length us, event | category | flops | bytes accessed | tf_op | source)
XLA Modules:
  0.0 133.2 jit_solution(5096519232398412909)
XLA Ops:
  7.5 2.2 %collective-permute-start = (f32[1,5,128,128]{3,2,1,0:T(8,128)S(1)}, f32[1,5,128,128]{3,2,1,0:T(8,128)S(1)}, u32[]{:S(2)}, u32[]{:S(2)}) collective-permute-start(f32[1,5,128,128]{3,2,1,0:T(8,128)S(1)} %slice_bitcast_fusion.2), channel_id=1, source_target_pairs={{0,64},{64,0},{128,192},{192,128},{1,65},{65,1},{129,193},{193,129... | collective-permute-start | bytes 983048 | tf_op jit(solution)/shard_map/ppermute | solution.py:372
  11.5 3.4 %slice_bitcast_fusion = (f32[5,5,128,128]{3,2,1,0:T(8,128)S(1)}, f32[5,5,128,128]{3,2,1,0:T(8,128)}) fusion(f32[1,2,1,5,1,5,128,128]{7,6,5,3,4,2,1,0:T(8,128)} %bitcast.35), kind=kLoop, calls=%fused_computation | loop fusion | bytes 6553600 | tf_op jit(solution)/shard_map/squeeze | solution.py:366
  16.7 1.5 %tile.1.refs_0_ = f32[128,128]{1,0:T(8,128)} custom-call(s32[2,2,8]{2,1,0:T(2,128)} %pad_add_fusion.pos, f32[8,8,128,128]{3,2,1,0:T(8,128)} %bitcast.30, f32[5,5,128,128]{3,2,1,0:T(8,128)} %get-tuple-element.80.own, f32[1,5,128,128]{3,2,1,0:T(8,128)} %copy-done), custom_call_target="tpu_custom_call" | custom-call | tf_op jit(solution)/shard_map/tile/pallas_call | solution.py:378
  18.2 2.3 %collective-permute-start.2 = (f32[4,128,128]{2,1,0:T(8,128)S(1)}, f32[4,128,128]{2,1,0:T(8,128)S(1)}, u32[]{:S(2)}, u32[]{:S(2)}) collective-permute-start(f32[4,128,128]{2,1,0:T(8,128)S(1)} %slice_bitcast_fusion.3), channel_id=1, source_target_pairs={{0,64},{64,0},{128,192},{192,128},{1,65},{65,1},{129,193},{193,129... | collective-permute-start | bytes 786440 | tf_op jit(solution)/shard_map/ppermute | solution.py:387
  20.5 3.7 %collective-permute-start.3 = (f32[128,128]{1,0:T(8,128)}, f32[128,128]{1,0:T(8,128)S(1)}, u32[]{:S(2)}, u32[]{:S(2)}) collective-permute-start(f32[128,128]{1,0:T(8,128)} %tile.1.refs_0_), channel_id=1, source_target_pairs={{0,8},{32,40},{24,32},{9,17},{1,9},{33,41},{18,26},{10,18},{2,10},... | collective-permute-start | bytes 196616 | tf_op jit(solution)/shard_map/ppermute | solution.py:408
  24.2 2.6 %collective-permute-start.4 = (f32[128,128]{1,0:T(8,128)}, f32[128,128]{1,0:T(8,128)S(1)}, u32[]{:S(2)}, u32[]{:S(2)}) collective-permute-start(f32[128,128]{1,0:T(8,128)} %tile.1.refs_0_), channel_id=1, source_target_pairs={{0,16},{32,48},{24,40},{9,25},{1,17},{33,49},{18,34},{10,26},{2,18... | collective-permute-start | bytes 196616 | tf_op jit(solution)/shard_map/ppermute | solution.py:408
  26.9 2.0 %collective-permute-start.5 = (f32[128,128]{1,0:T(8,128)}, f32[128,128]{1,0:T(8,128)S(1)}, u32[]{:S(2)}, u32[]{:S(2)}) collective-permute-start(f32[128,128]{1,0:T(8,128)} %tile.1.refs_0_), channel_id=1, source_target_pairs={{0,24},{32,56},{24,48},{9,33},{1,25},{33,57},{18,42},{10,34},{2,26... | collective-permute-start | bytes 196616 | tf_op jit(solution)/shard_map/ppermute | solution.py:408
  28.9 6.5 %collective-permute-start.6 = (f32[128,128]{1,0:T(8,128)}, f32[128,128]{1,0:T(8,128)S(1)}, u32[]{:S(2)}, u32[]{:S(2)}) collective-permute-start(f32[128,128]{1,0:T(8,128)} %tile.1.refs_0_), channel_id=1, source_target_pairs={{0,32},{32,0},{24,56},{9,41},{1,33},{33,1},{18,50},{10,42},{2,34},... | collective-permute-start | bytes 196616 | tf_op jit(solution)/shard_map/ppermute | solution.py:408
  35.4 1.3 collective-permute-start.7
  36.7 1.3 collective-permute-start.8
  38.1 1.9 %collective-permute-start.9 = (f32[128,128]{1,0:T(8,128)}, f32[128,128]{1,0:T(8,128)S(1)}, u32[]{:S(2)}, u32[]{:S(2)}) collective-permute-start(f32[128,128]{1,0:T(8,128)} %tile.1.refs_0_), channel_id=1, source_target_pairs={{0,56},{32,24},{24,16},{9,1},{1,57},{33,25},{18,10},{10,2},{2,58},... | collective-permute-start | bytes 196616 | tf_op jit(solution)/shard_map/ppermute | solution.py:408
  40.0 2.2 %row_panel.1 = f32[8,128,128]{2,1,0:T(8,128)} custom-call(s32[2,2,8]{2,1,0:T(2,128)} %pad_add_fusion.pos, f32[8,8,128,128]{3,2,1,0:T(8,128)} %bitcast.31, f32[5,5,128,128]{3,2,1,0:T(8,128)} %get-tuple-element.80.own, f32[1,5,128,128]{3,2,1,0:T(8,128)} %copy-done), custom_call_target="tpu_custom_call" | custom-call | tf_op jit(solution)/shard_map/row_panel/pallas_call | solution.py:389
  44.0 1.9 %pick.1 = f32[3,128,128]{2,1,0:T(8,128)} custom-call(s32[2]{0:T(128)} %pad_add_fusion.2.place, f32[128,128]{1,0:T(8,128)} %tile.1.refs_0_, f32[128,128]{1,0:T(8,128)} %copy-done.11, f32[128,128]{1,0:T(8,128)} %copy-done.12, f32[128,128]{1,0:T(8,128)} %copy-done.13, f32[128,128]{1,0:T(8,128)} %copy-done.14, f32[128,128]{1,0:T(8,128)} %copy-done.15, ...), custom_call_target="tpu_custom_call" | custom-call | tf_op jit(solution)/shard_map/pick/pallas_call | solution.py:411
  45.9 5.5 %collective-permute-start.10 = (f32[3,128,128]{2,1,0:T(8,128)}, f32[3,128,128]{2,1,0:T(8,128)S(1)}, u32[]{:S(2)}, u32[]{:S(2)}) collective-permute-start(f32[3,128,128]{2,1,0:T(8,128)} %pick.1), channel_id=1, source_target_pairs={{0,2},{1,3},{2,4},{3,5},{4,6},{8,10},{9,11},{10,12},{11,13},{12,14... | collective-permute-start | bytes 589832 | tf_op jit(solution)/shard_map/ppermute | solution.py:436
  51.4 1.3 collective-permute-start.11
  52.7 1.9 %collective-permute-start.12 = (f32[3,128,128]{2,1,0:T(8,128)}, f32[3,128,128]{2,1,0:T(8,128)S(1)}, u32[]{:S(2)}, u32[]{:S(2)}) collective-permute-start(f32[3,128,128]{2,1,0:T(8,128)} %pick.1), channel_id=1, source_target_pairs={{0,6},{1,7},{2,0},{3,1},{4,2},{8,14},{9,15},{10,8},{11,9},{12,10},... | collective-permute-start | bytes 589832 | tf_op jit(solution)/shard_map/ppermute | solution.py:436
  54.7 2.3 %col_panel.1.m0 = f32[8,128,128]{2,1,0:T(8,128)} custom-call(s32[2,2,8]{2,1,0:T(2,128)} %pad_add_fusion.pos, f32[8,8,128,128]{3,2,1,0:T(8,128)} %bitcast.32, f32[5,5,128,128]{3,2,1,0:T(8,128)} %get-tuple-element.80.own, f32[1,5,128,128]{3,2,1,0:T(8,128)} %copy-done, f32[4,128,128]{2,1,0:T(8,128)} %copy-done.10), custom_call_target="tpu_custom_call" | custom-call | tf_op jit(solution)/shard_map/col_panel/pallas_call | solution.py:419
  57.0 2.7 %collective-permute-done.11 = f32[3,128,128]{2,1,0:T(8,128)S(1)} collective-permute-done((f32[3,128,128]{2,1,0:T(8,128)}, f32[3,128,128]{2,1,0:T(8,128)S(1)}, u32[]{:S(2)}, u32[]{:S(2)}) %collective-permute-start.11) | collective-permute-done | bytes 196640 | tf_op jit(solution)/shard_map/ppermute | solution.py:436
  59.7 1.9 %collective-permute-done.12 = f32[3,128,128]{2,1,0:T(8,128)S(1)} collective-permute-done((f32[3,128,128]{2,1,0:T(8,128)}, f32[3,128,128]{2,1,0:T(8,128)S(1)}, u32[]{:S(2)}, u32[]{:S(2)}) %collective-permute-start.12) | collective-permute-done | bytes 196640 | tf_op jit(solution)/shard_map/ppermute | solution.py:436
  61.7 1.4 %collective-permute-start.16 = (f32[4,3,128,128]{3,2,1,0:T(8,128)S(1)}, f32[4,3,128,128]{3,2,1,0:T(8,128)S(1)}, u32[]{:S(2)}, u32[]{:S(2)}) collective-permute-start(f32[4,3,128,128]{3,2,1,0:T(8,128)S(1)} %pad_maximum_fusion.mine), channel_id=1, source_target_pairs={{0,1},{1,0},{2,3},{3,2},{4,5},{5,4},{6,7},{7,6},{8,9},{9,8},{10,11... | collective-permute-start | bytes 2359304 | tf_op jit(solution)/shard_map/ppermute | solution.py:444
  63.5 1.4 %collective-permute-start.13 = (f32[8,128,128]{2,1,0:T(8,128)S(1)}, f32[8,128,128]{2,1,0:T(8,128)S(1)}, u32[]{:S(2)}, u32[]{:S(2)}) collective-permute-start(f32[8,128,128]{2,1,0:T(8,128)S(1)} %copy-done.4), channel_id=1, source_target_pairs={{0,2},{1,3},{2,4},{3,5},{4,6},{8,10},{9,11},{10,12},{11,13},{12,14... | collective-permute-start | bytes 1572872 | tf_op jit(solution)/shard_map/ppermute | solution.py:441
  64.9 3.5 %collective-permute-start.14 = (f32[8,128,128]{2,1,0:T(8,128)S(1)}, f32[8,128,128]{2,1,0:T(8,128)S(1)}, u32[]{:S(2)}, u32[]{:S(2)}) collective-permute-start(f32[8,128,128]{2,1,0:T(8,128)S(1)} %copy-done.4), channel_id=1, source_target_pairs={{0,4},{1,5},{2,6},{3,7},{4,0},{8,12},{9,13},{10,14},{11,15},{12,8}... | collective-permute-start | bytes 1572872 | tf_op jit(solution)/shard_map/ppermute | solution.py:441
  68.4 1.9 %collective-permute-start.15 = (f32[8,128,128]{2,1,0:T(8,128)S(1)}, f32[8,128,128]{2,1,0:T(8,128)S(1)}, u32[]{:S(2)}, u32[]{:S(2)}) collective-permute-start(f32[8,128,128]{2,1,0:T(8,128)S(1)} %copy-done.4), channel_id=1, source_target_pairs={{0,6},{1,7},{2,0},{3,1},{4,2},{8,14},{9,15},{10,8},{11,9},{12,10},... | collective-permute-start | bytes 1572872 | tf_op jit(solution)/shard_map/ppermute | solution.py:441
  70.3 3.9 %collective-permute-start.17 = (f32[8,128,128]{2,1,0:T(8,128)S(1)}, f32[8,128,128]{2,1,0:T(8,128)S(1)}, u32[]{:S(2)}, u32[]{:S(2)}) collective-permute-start(f32[8,128,128]{2,1,0:T(8,128)S(1)} %copy-done.4), channel_id=1, source_target_pairs={{0,1},{1,0},{2,3},{3,2},{4,5},{5,4},{6,7},{7,6},{8,9},{9,8},{10,11... | collective-permute-start | bytes 1572872 | tf_op jit(solution)/shard_map/ppermute | solution.py:462
  74.3 14.3 %head.1 = (f32[384,640]{1,0:T(8,128)S(1)}, f32[3,128,128]{2,1,0:T(8,128)S(1)}, f32[256,640]{1,0:T(8,128)S(1)}) custom-call(s32[2]{0:T(128)S(1)} %copy-done.8, f32[4,3,128,128]{3,2,1,0:T(8,128)S(1)} %pad_maximum_fusion.mine, f32[4,3,128,128]{3,2,1,0:T(8,128)S(1)} %collective-permute-done.16.other), custom_call_target="tpu_custom_call" | custom-call | flops 17999998976 | bytes 6000000 | tf_op jit(solution)/shard_map/head/pallas_call | solution.py:445
  88.6 3.3 %collective-permute-done.15.m3 = f32[8,128,128]{2,1,0:T(8,128)S(1)} collective-permute-done((f32[8,128,128]{2,1,0:T(8,128)S(1)}, f32[8,128,128]{2,1,0:T(8,128)S(1)}, u32[]{:S(2)}, u32[]{:S(2)}) %collective-permute-start.15) | collective-permute-done | bytes 524320 | tf_op jit(solution)/shard_map/ppermute | solution.py:441
  91.8 1.6 %collective-permute-start.18 = (f32[8,128,128]{2,1,0:T(8,128)S(1)}, f32[8,128,128]{2,1,0:T(8,128)S(1)}, u32[]{:S(2)}, u32[]{:S(2)}) collective-permute-start(f32[8,128,128]{2,1,0:T(8,128)S(1)} %collective-permute-done.13.m1), channel_id=1, source_target_pairs={{0,1},{1,0},{2,3},{3,2},{4,5},{5,4},{6,7},{7,6},{8,9},{9,8},{10,11... | collective-permute-start | bytes 1572872 | tf_op jit(solution)/shard_map/ppermute | solution.py:462
  93.9 4.4 %middle.1 = (f32[128,640]{1,0:T(8,128)S(1)}, f32[1,128,128]{2,1,0:T(8,128)S(1)}, f32[128,640]{1,0:T(8,128)S(1)}) custom-call(f32[256,640]{1,0:T(8,128)S(1)} %get-tuple-element.56.rest), custom_call_target="tpu_custom_call" | custom-call | flops 6000000000 | bytes 2000000 | tf_op jit(solution)/shard_map/middle/pallas_call | solution.py:463
  98.4 8.2 %tail.1 = (f32[640,640]{1,0:T(8,128)S(1)}, f32[5,128,128]{2,1,0:T(8,128)S(1)}, bf16[1024,640]{1,0:T(8,128)(2,1)S(1)}, bf16[1024,640]{1,0:T(8,128)(2,1)S(1)}, f32[8,128,128]{2,1,0:T(8,128)S(1)}) custom-call(s32[2]{0:T(128)S(1)} %copy-done.8, f32[128,640]{1,0:T(8,128)S(1)} %get-tuple-element.60.rest, f32[384,640]{1,0:T(8,128)S(1)} %get-tuple-element.61.head_inverse, ...), custom_call_target="tpu_custom_call" | custom-call | flops 8999999488 | bytes 6000000 | tf_op jit(solution)/shard_map/tail/pallas_call | solution.py:476
  106.6 1.2 copy-done.2
  107.8 1.1 copy-done.3
  110.6 15.7 %schur.1 = f32[8,8,128,128]{3,2,1,0:T(8,128)} custom-call(s32[2,2,8]{2,1,0:T(2,128)S(1)} %copy-done.7, s32[2]{0:T(128)S(1)} %copy-done.8, f32[8,8,128,128]{3,2,1,0:T(8,128)} %bitcast.33, f32[5,5,128,128]{3,2,1,0:T(8,128)} %get-tuple-element.80.own, f32[1,5,128,128]{3,2,1,0:T(8,128)S(1)} %copy-done.1, f32[4,5,128,128]{3,2,1,0:T(8,128)S(1)} %collective-permute-done.1.below, ...), custom_call_target="tpu_custom_call" | custom-call | tf_op jit(solution)/shard_map/schur/pallas_call | solution.py:499
  (73 shorter events, 8.8 us)
Async XLA Ops:
  6.5 103.1 %all-gather.3.cloned.1.call-start = ((), (), s32[]{:S(2)}) async-start(), calls=%async_computation | async-start | bytes 4718592 | tf_op jit(solution)/shard_map/all_gather | solution.py:410
  7.5 8.4 %collective-permute-start = (f32[1,5,128,128]{3,2,1,0:T(8,128)S(1)}, f32[1,5,128,128]{3,2,1,0:T(8,128)S(1)}, u32[]{:S(2)}, u32[]{:S(2)}) collective-permute-start(f32[1,5,128,128]{3,2,1,0:T(8,128)S(1)} %slice_bitcast_fusion.2), channel_id=1, source_target_pairs={{0,64},{64,0},{128,192},{192,128},{1,65},{65,1},{129,193},{193,129... | collective-permute-start | bytes 983048 | tf_op jit(solution)/shard_map/ppermute | solution.py:372
  18.2 25.1 %collective-permute-start.2 = (f32[4,128,128]{2,1,0:T(8,128)S(1)}, f32[4,128,128]{2,1,0:T(8,128)S(1)}, u32[]{:S(2)}, u32[]{:S(2)}) collective-permute-start(f32[4,128,128]{2,1,0:T(8,128)S(1)} %slice_bitcast_fusion.3), channel_id=1, source_target_pairs={{0,64},{64,0},{128,192},{192,128},{1,65},{65,1},{129,193},{193,129... | collective-permute-start | bytes 786440 | tf_op jit(solution)/shard_map/ppermute | solution.py:387
  20.5 14.9 %collective-permute-start.3 = (f32[128,128]{1,0:T(8,128)}, f32[128,128]{1,0:T(8,128)S(1)}, u32[]{:S(2)}, u32[]{:S(2)}) collective-permute-start(f32[128,128]{1,0:T(8,128)} %tile.1.refs_0_), channel_id=1, source_target_pairs={{0,8},{32,40},{24,32},{9,17},{1,9},{33,41},{18,26},{10,18},{2,10},... | collective-permute-start | bytes 196616 | tf_op jit(solution)/shard_map/ppermute | solution.py:408
  24.2 12.5 %collective-permute-start.4 = (f32[128,128]{1,0:T(8,128)}, f32[128,128]{1,0:T(8,128)S(1)}, u32[]{:S(2)}, u32[]{:S(2)}) collective-permute-start(f32[128,128]{1,0:T(8,128)} %tile.1.refs_0_), channel_id=1, source_target_pairs={{0,16},{32,48},{24,40},{9,25},{1,17},{33,49},{18,34},{10,26},{2,18... | collective-permute-start | bytes 196616 | tf_op jit(solution)/shard_map/ppermute | solution.py:408
  26.9 11.1 %collective-permute-start.5 = (f32[128,128]{1,0:T(8,128)}, f32[128,128]{1,0:T(8,128)S(1)}, u32[]{:S(2)}, u32[]{:S(2)}) collective-permute-start(f32[128,128]{1,0:T(8,128)} %tile.1.refs_0_), channel_id=1, source_target_pairs={{0,24},{32,56},{24,48},{9,33},{1,25},{33,57},{18,42},{10,34},{2,26... | collective-permute-start | bytes 196616 | tf_op jit(solution)/shard_map/ppermute | solution.py:408
  28.9 13.3 %collective-permute-start.6 = (f32[128,128]{1,0:T(8,128)}, f32[128,128]{1,0:T(8,128)S(1)}, u32[]{:S(2)}, u32[]{:S(2)}) collective-permute-start(f32[128,128]{1,0:T(8,128)} %tile.1.refs_0_), channel_id=1, source_target_pairs={{0,32},{32,0},{24,56},{9,41},{1,33},{33,1},{18,50},{10,42},{2,34},... | collective-permute-start | bytes 196616 | tf_op jit(solution)/shard_map/ppermute | solution.py:408
  35.4 6.8 %copy-start.11 = (f32[128,128]{1,0:T(8,128)}, f32[128,128]{1,0:T(8,128)S(1)}, u32[]{:S(2)}) copy-start(f32[128,128]{1,0:T(8,128)S(1)} %collective-permute-done.3.refs_1_) | copy-start | bytes 196612
  35.4 6.8 %collective-permute-start.7 = (f32[128,128]{1,0:T(8,128)}, f32[128,128]{1,0:T(8,128)S(1)}, u32[]{:S(2)}, u32[]{:S(2)}) collective-permute-start(f32[128,128]{1,0:T(8,128)} %tile.1.refs_0_), channel_id=1, source_target_pairs={{0,40},{32,8},{24,0},{9,49},{1,41},{33,9},{18,58},{10,50},{2,42},{... | collective-permute-start | bytes 196616 | tf_op jit(solution)/shard_map/ppermute | solution.py:408
  36.7 5.5 %copy-start.12 = (f32[128,128]{1,0:T(8,128)}, f32[128,128]{1,0:T(8,128)S(1)}, u32[]{:S(2)}) copy-start(f32[128,128]{1,0:T(8,128)S(1)} %collective-permute-done.4.refs_2_) | copy-start | bytes 196612
  36.7 5.5 %collective-permute-start.8 = (f32[128,128]{1,0:T(8,128)}, f32[128,128]{1,0:T(8,128)S(1)}, u32[]{:S(2)}, u32[]{:S(2)}) collective-permute-start(f32[128,128]{1,0:T(8,128)} %tile.1.refs_0_), channel_id=1, source_target_pairs={{0,48},{32,16},{24,8},{9,57},{1,49},{33,17},{18,2},{10,58},{2,50},... | collective-permute-start | bytes 196616 | tf_op jit(solution)/shard_map/ppermute | solution.py:408
  38.1 4.2 %copy-start.13 = (f32[128,128]{1,0:T(8,128)}, f32[128,128]{1,0:T(8,128)S(1)}, u32[]{:S(2)}) copy-start(f32[128,128]{1,0:T(8,128)S(1)} %collective-permute-done.5.refs_3_) | copy-start | bytes 196612
  38.1 5.2 %collective-permute-start.9 = (f32[128,128]{1,0:T(8,128)}, f32[128,128]{1,0:T(8,128)S(1)}, u32[]{:S(2)}, u32[]{:S(2)}) collective-permute-start(f32[128,128]{1,0:T(8,128)} %tile.1.refs_0_), channel_id=1, source_target_pairs={{0,56},{32,24},{24,16},{9,1},{1,57},{33,25},{18,10},{10,2},{2,58},... | collective-permute-start | bytes 196616 | tf_op jit(solution)/shard_map/ppermute | solution.py:408
  42.3 1.7 %copy-start.14 = (f32[128,128]{1,0:T(8,128)}, f32[128,128]{1,0:T(8,128)S(1)}, u32[]{:S(2)}) copy-start(f32[128,128]{1,0:T(8,128)S(1)} %collective-permute-done.6.refs_4_) | copy-start | bytes 196612
  43.3 11.4 %copy-start.10 = (f32[4,128,128]{2,1,0:T(8,128)}, f32[4,128,128]{2,1,0:T(8,128)S(1)}, u32[]{:S(2)}) copy-start(f32[4,128,128]{2,1,0:T(8,128)S(1)} %collective-permute-done.2.below) | copy-start | bytes 786436
  45.9 15.8 %copy-start.9 = (f32[3,128,128]{2,1,0:T(8,128)S(1)}, f32[3,128,128]{2,1,0:T(8,128)}, u32[]{:S(2)}) copy-start(f32[3,128,128]{2,1,0:T(8,128)} %pick.1) | copy-start | bytes 589828
  45.9 11.1 %collective-permute-start.10 = (f32[3,128,128]{2,1,0:T(8,128)}, f32[3,128,128]{2,1,0:T(8,128)S(1)}, u32[]{:S(2)}, u32[]{:S(2)}) collective-permute-start(f32[3,128,128]{2,1,0:T(8,128)} %pick.1), channel_id=1, source_target_pairs={{0,2},{1,3},{2,4},{3,5},{4,6},{8,10},{9,11},{10,12},{11,13},{12,14... | collective-permute-start | bytes 589832 | tf_op jit(solution)/shard_map/ppermute | solution.py:436
  51.4 8.3 %collective-permute-start.11 = (f32[3,128,128]{2,1,0:T(8,128)}, f32[3,128,128]{2,1,0:T(8,128)S(1)}, u32[]{:S(2)}, u32[]{:S(2)}) collective-permute-start(f32[3,128,128]{2,1,0:T(8,128)} %pick.1), channel_id=1, source_target_pairs={{0,4},{1,5},{2,6},{3,7},{4,0},{8,12},{9,13},{10,14},{11,15},{12,8}... | collective-permute-start | bytes 589832 | tf_op jit(solution)/shard_map/ppermute | solution.py:436
  52.7 8.9 %collective-permute-start.12 = (f32[3,128,128]{2,1,0:T(8,128)}, f32[3,128,128]{2,1,0:T(8,128)S(1)}, u32[]{:S(2)}, u32[]{:S(2)}) collective-permute-start(f32[3,128,128]{2,1,0:T(8,128)} %pick.1), channel_id=1, source_target_pairs={{0,6},{1,7},{2,0},{3,1},{4,2},{8,14},{9,15},{10,8},{11,9},{12,10},... | collective-permute-start | bytes 589832 | tf_op jit(solution)/shard_map/ppermute | solution.py:436
  61.7 1.8 %copy-start.4 = (f32[8,128,128]{2,1,0:T(8,128)S(1)}, f32[8,128,128]{2,1,0:T(8,128)}, u32[]{:S(2)}) copy-start(f32[8,128,128]{2,1,0:T(8,128)} %col_panel.1.m0) | copy-start | bytes 1572868
  61.7 12.6 %copy-start.8 = (s32[2]{0:T(128)S(1)}, s32[2]{0:T(128)}, u32[]{:S(2)}) copy-start(s32[2]{0:T(128)} %pad_add_fusion.2.place) | copy-start | bytes 28
  61.7 8.6 %collective-permute-start.16 = (f32[4,3,128,128]{3,2,1,0:T(8,128)S(1)}, f32[4,3,128,128]{3,2,1,0:T(8,128)S(1)}, u32[]{:S(2)}, u32[]{:S(2)}) collective-permute-start(f32[4,3,128,128]{3,2,1,0:T(8,128)S(1)} %pad_maximum_fusion.mine), channel_id=1, source_target_pairs={{0,1},{1,0},{2,3},{3,2},{4,5},{5,4},{6,7},{7,6},{8,9},{9,8},{10,11... | collective-permute-start | bytes 2359304 | tf_op jit(solution)/shard_map/ppermute | solution.py:444
  63.2 35.1 %collective-permute-start.1 = (f32[4,5,128,128]{3,2,1,0:T(8,128)S(1)}, f32[4,5,128,128]{3,2,1,0:T(8,128)S(1)}, u32[]{:S(2)}, u32[]{:S(2)}) collective-permute-start(f32[4,5,128,128]{3,2,1,0:T(8,128)S(1)} %slice.23), channel_id=1, source_target_pairs={{0,64},{64,0},{128,192},{192,128},{1,65},{65,1},{129,193},{193,129... | collective-permute-start | bytes 3932168 | tf_op jit(solution)/shard_map/ppermute | solution.py:388
  63.5 25.1 %collective-permute-start.13 = (f32[8,128,128]{2,1,0:T(8,128)S(1)}, f32[8,128,128]{2,1,0:T(8,128)S(1)}, u32[]{:S(2)}, u32[]{:S(2)}) collective-permute-start(f32[8,128,128]{2,1,0:T(8,128)S(1)} %copy-done.4), channel_id=1, source_target_pairs={{0,2},{1,3},{2,4},{3,5},{4,6},{8,10},{9,11},{10,12},{11,13},{12,14... | collective-permute-start | bytes 1572872 | tf_op jit(solution)/shard_map/ppermute | solution.py:441
  64.9 23.7 %collective-permute-start.14 = (f32[8,128,128]{2,1,0:T(8,128)S(1)}, f32[8,128,128]{2,1,0:T(8,128)S(1)}, u32[]{:S(2)}, u32[]{:S(2)}) collective-permute-start(f32[8,128,128]{2,1,0:T(8,128)S(1)} %copy-done.4), channel_id=1, source_target_pairs={{0,4},{1,5},{2,6},{3,7},{4,0},{8,12},{9,13},{10,14},{11,15},{12,8}... | collective-permute-start | bytes 1572872 | tf_op jit(solution)/shard_map/ppermute | solution.py:441
  68.4 23.4 %collective-permute-start.15 = (f32[8,128,128]{2,1,0:T(8,128)S(1)}, f32[8,128,128]{2,1,0:T(8,128)S(1)}, u32[]{:S(2)}, u32[]{:S(2)}) collective-permute-start(f32[8,128,128]{2,1,0:T(8,128)S(1)} %copy-done.4), channel_id=1, source_target_pairs={{0,6},{1,7},{2,0},{3,1},{4,2},{8,14},{9,15},{10,8},{11,9},{12,10},... | collective-permute-start | bytes 1572872 | tf_op jit(solution)/shard_map/ppermute | solution.py:441
  70.3 28.0 %collective-permute-start.17 = (f32[8,128,128]{2,1,0:T(8,128)S(1)}, f32[8,128,128]{2,1,0:T(8,128)S(1)}, u32[]{:S(2)}, u32[]{:S(2)}) collective-permute-start(f32[8,128,128]{2,1,0:T(8,128)S(1)} %copy-done.4), channel_id=1, source_target_pairs={{0,1},{1,0},{2,3},{3,2},{4,5},{5,4},{6,7},{7,6},{8,9},{9,8},{10,11... | collective-permute-start | bytes 1572872 | tf_op jit(solution)/shard_map/ppermute | solution.py:462
  91.8 6.5 %collective-permute-start.18 = (f32[8,128,128]{2,1,0:T(8,128)S(1)}, f32[8,128,128]{2,1,0:T(8,128)S(1)}, u32[]{:S(2)}, u32[]{:S(2)}) collective-permute-start(f32[8,128,128]{2,1,0:T(8,128)S(1)} %collective-permute-done.13.m1), channel_id=1, source_target_pairs={{0,1},{1,0},{2,3},{3,2},{4,5},{5,4},{6,7},{7,6},{8,9},{9,8},{10,11... | collective-permute-start | bytes 1572872 | tf_op jit(solution)/shard_map/ppermute | solution.py:462
  93.4 5.0 %collective-permute-start.19 = (f32[8,128,128]{2,1,0:T(8,128)S(1)}, f32[8,128,128]{2,1,0:T(8,128)S(1)}, u32[]{:S(2)}, u32[]{:S(2)}) collective-permute-start(f32[8,128,128]{2,1,0:T(8,128)S(1)} %collective-permute-done.14.m2), channel_id=1, source_target_pairs={{0,1},{1,0},{2,3},{3,2},{4,5},{5,4},{6,7},{7,6},{8,9},{9,8},{10,11... | collective-permute-start | bytes 1572872 | tf_op jit(solution)/shard_map/ppermute | solution.py:462
  93.4 5.0 %collective-permute-start.20 = (f32[8,128,128]{2,1,0:T(8,128)S(1)}, f32[8,128,128]{2,1,0:T(8,128)S(1)}, u32[]{:S(2)}, u32[]{:S(2)}) collective-permute-start(f32[8,128,128]{2,1,0:T(8,128)S(1)} %collective-permute-done.15.m3), channel_id=1, source_target_pairs={{0,1},{1,0},{2,3},{3,2},{4,5},{5,4},{6,7},{7,6},{8,9},{9,8},{10,11... | collective-permute-start | bytes 1572872 | tf_op jit(solution)/shard_map/ppermute | solution.py:462
  98.4 11.3 %copy-start.1 = (f32[1,5,128,128]{3,2,1,0:T(8,128)S(1)}, f32[1,5,128,128]{3,2,1,0:T(8,128)}, u32[]{:S(2)}) copy-start(f32[1,5,128,128]{3,2,1,0:T(8,128)} %copy-done) | copy-start | bytes 983044
  98.4 11.2 %copy-start.7 = (s32[2,2,8]{2,1,0:T(2,128)S(1)}, s32[2,2,8]{2,1,0:T(2,128)}, u32[]{:S(2)}) copy-start(s32[2,2,8]{2,1,0:T(2,128)} %pad_add_fusion.pos) | copy-start | bytes 388
  (8 other events, 8.7 us)
Sparse Core Ops, SparseCore 0:
  43.4 56.3 all-gather.2

commit v2 on v1

--- a/solution.py
+++ b/solution.py
@@ -202,9 +202,18 @@
         for start, stop in CUTS[:-1]
         for rows in quarters
     ]
+    done = LAST * TILE
+
+    def reduce(rows):
+        known = work[span(LAST), LEAD : LEAD + done]
+        full[rows, done:] = panel[rows, done:] + mul_nt(panel[rows, :done], known)
+
+    beside += [functools.partial(reduce, rows) for rows in quarters]
     advance(work, diagonal_ref, LAST, beside)
     keep_inverse(work, inverse_ref, LAST)
-    product(slice(0, 8 * TILE), *CUTS[-1])
+    part = mul_nt(full[:, done:], inverse_ref[done:, done:])
+    high[:, done:], low[:, done:] = split(part)
+    full[:, done:] = part
     wanted = jnp.minimum(column, PANELS - 1)
     for k in range(PANELS):
 

time: 134 us -> 134 us (level)
  no operation moved by 1% of the time
where the time goes in v2:
time: 134 us; the launch traced here: 133 us
  Pallas kernels  50.5 us (38%)
  starting transfers between devices  47.1 us (35%)
  between operations  13.8 us (10%)
  local copies, waits for them, and re-layouts  10 us (7%)
  waiting for transfers between devices  9.93 us (7%)
  other arithmetic  1.69 us (1%)
    ppermute x7, starting transfers between devices, per_device(): found.append(lax.ppermute(tile, both, step))  19.4 us
    pallas_call x1, Pallas kernels, per_device(): pl.pallas_call(schur_kernel, grid=(8 // WIDTH,), out_shape=f32(8, 8, TILE...  15.7 us
    pallas_call x1, Pallas kernels, per_device(): pl.pallas_call(head_kernel, out_shape=[f32(HEAD * TILE, LEAD), f32(HEAD,...  14.3 us
    ppermute x3, starting transfers between devices, per_device(): lax.ppermute(picked, 'col', [(c, (c + away) % 8) for c in range(PANELS)])  8.75 us
    pallas_call x1, Pallas kernels, per_device(): pl.pallas_call(tail_kernel, out_shape=[f32(LEAD, LEAD), f32(PANELS, TILE,...  8.03 us
    ppermute x3, starting transfers between devices, per_device(): lax.ppermute(col_panel, 'col', [(c, (c + away) % 8) for c in range(PANELS)])  6.8 us
    ppermute x4, starting transfers between devices, per_device(): col_other = [lax.ppermute(part, 'col', across) for part in col_mine]  5.98 us
    unnamed x36, local copies, waits for them, and re-layouts  4.79 us
  transfers between devices with their start and end apart: 22, of which 5 were waited for; matrix products, arithmetic and copies ran while one was open for 4% of the time, Pallas kernels for 25%

profile of v2, /device:TPU:1, one launch (start us, length us, event | category | flops | bytes accessed | tf_op | source)
XLA Modules:
  0.0 133.0 jit_solution(16791451107068225323)
XLA Ops:
  7.5 2.2 %collective-permute-start = (f32[1,5,128,128]{3,2,1,0:T(8,128)S(1)}, f32[1,5,128,128]{3,2,1,0:T(8,128)S(1)}, u32[]{:S(2)}, u32[]{:S(2)}) collective-permute-start(f32[1,5,128,128]{3,2,1,0:T(8,128)S(1)} %slice_bitcast_fusion.2), channel_id=1, source_target_pairs={{0,64},{64,0},{128,192},{192,128},{1,65},{65,1},{129,193},{193,129... | collective-permute-start | bytes 983048 | tf_op jit(solution)/shard_map/ppermute | solution.py:381
  11.5 3.4 %slice_bitcast_fusion = (f32[5,5,128,128]{3,2,1,0:T(8,128)S(1)}, f32[5,5,128,128]{3,2,1,0:T(8,128)}) fusion(f32[1,2,1,5,1,5,128,128]{7,6,5,3,4,2,1,0:T(8,128)} %bitcast.35), kind=kLoop, calls=%fused_computation | loop fusion | bytes 6553600 | tf_op jit(solution)/shard_map/squeeze | solution.py:375
  16.7 1.5 %tile.1.refs_0_ = f32[128,128]{1,0:T(8,128)} custom-call(s32[2,2,8]{2,1,0:T(2,128)} %pad_add_fusion.pos, f32[8,8,128,128]{3,2,1,0:T(8,128)} %bitcast.30, f32[5,5,128,128]{3,2,1,0:T(8,128)} %get-tuple-element.80.own, f32[1,5,128,128]{3,2,1,0:T(8,128)} %copy-done), custom_call_target="tpu_custom_call" | custom-call | tf_op jit(solution)/shard_map/tile/pallas_call | solution.py:387
  18.2 2.3 %collective-permute-start.2 = (f32[4,128,128]{2,1,0:T(8,128)S(1)}, f32[4,128,128]{2,1,0:T(8,128)S(1)}, u32[]{:S(2)}, u32[]{:S(2)}) collective-permute-start(f32[4,128,128]{2,1,0:T(8,128)S(1)} %slice_bitcast_fusion.3), channel_id=1, source_target_pairs={{0,64},{64,0},{128,192},{192,128},{1,65},{65,1},{129,193},{193,129... | collective-permute-start | bytes 786440 | tf_op jit(solution)/shard_map/ppermute | solution.py:396
  20.5 3.7 %collective-permute-start.3 = (f32[128,128]{1,0:T(8,128)}, f32[128,128]{1,0:T(8,128)S(1)}, u32[]{:S(2)}, u32[]{:S(2)}) collective-permute-start(f32[128,128]{1,0:T(8,128)} %tile.1.refs_0_), channel_id=1, source_target_pairs={{0,8},{32,40},{24,32},{9,17},{1,9},{33,41},{18,26},{10,18},{2,10},... | collective-permute-start | bytes 196616 | tf_op jit(solution)/shard_map/ppermute | solution.py:417
  24.2 2.6 %collective-permute-start.4 = (f32[128,128]{1,0:T(8,128)}, f32[128,128]{1,0:T(8,128)S(1)}, u32[]{:S(2)}, u32[]{:S(2)}) collective-permute-start(f32[128,128]{1,0:T(8,128)} %tile.1.refs_0_), channel_id=1, source_target_pairs={{0,16},{32,48},{24,40},{9,25},{1,17},{33,49},{18,34},{10,26},{2,18... | collective-permute-start | bytes 196616 | tf_op jit(solution)/shard_map/ppermute | solution.py:417
  26.9 2.0 %collective-permute-start.5 = (f32[128,128]{1,0:T(8,128)}, f32[128,128]{1,0:T(8,128)S(1)}, u32[]{:S(2)}, u32[]{:S(2)}) collective-permute-start(f32[128,128]{1,0:T(8,128)} %tile.1.refs_0_), channel_id=1, source_target_pairs={{0,24},{32,56},{24,48},{9,33},{1,25},{33,57},{18,42},{10,34},{2,26... | collective-permute-start | bytes 196616 | tf_op jit(solution)/shard_map/ppermute | solution.py:417
  28.9 6.5 %collective-permute-start.6 = (f32[128,128]{1,0:T(8,128)}, f32[128,128]{1,0:T(8,128)S(1)}, u32[]{:S(2)}, u32[]{:S(2)}) collective-permute-start(f32[128,128]{1,0:T(8,128)} %tile.1.refs_0_), channel_id=1, source_target_pairs={{0,32},{32,0},{24,56},{9,41},{1,33},{33,1},{18,50},{10,42},{2,34},... | collective-permute-start | bytes 196616 | tf_op jit(solution)/shard_map/ppermute | solution.py:417
  35.4 1.3 collective-permute-start.7
  36.7 1.3 collective-permute-start.8
  38.1 1.9 %collective-permute-start.9 = (f32[128,128]{1,0:T(8,128)}, f32[128,128]{1,0:T(8,128)S(1)}, u32[]{:S(2)}, u32[]{:S(2)}) collective-permute-start(f32[128,128]{1,0:T(8,128)} %tile.1.refs_0_), channel_id=1, source_target_pairs={{0,56},{32,24},{24,16},{9,1},{1,57},{33,25},{18,10},{10,2},{2,58},... | collective-permute-start | bytes 196616 | tf_op jit(solution)/shard_map/ppermute | solution.py:417
  40.0 2.2 %row_panel.1 = f32[8,128,128]{2,1,0:T(8,128)} custom-call(s32[2,2,8]{2,1,0:T(2,128)} %pad_add_fusion.pos, f32[8,8,128,128]{3,2,1,0:T(8,128)} %bitcast.31, f32[5,5,128,128]{3,2,1,0:T(8,128)} %get-tuple-element.80.own, f32[1,5,128,128]{3,2,1,0:T(8,128)} %copy-done), custom_call_target="tpu_custom_call" | custom-call | tf_op jit(solution)/shard_map/row_panel/pallas_call | solution.py:398
  44.0 1.9 %pick.1 = f32[3,128,128]{2,1,0:T(8,128)} custom-call(s32[2]{0:T(128)} %pad_add_fusion.2.place, f32[128,128]{1,0:T(8,128)} %tile.1.refs_0_, f32[128,128]{1,0:T(8,128)} %copy-done.11, f32[128,128]{1,0:T(8,128)} %copy-done.12, f32[128,128]{1,0:T(8,128)} %copy-done.13, f32[128,128]{1,0:T(8,128)} %copy-done.14, f32[128,128]{1,0:T(8,128)} %copy-done.15, ...), custom_call_target="tpu_custom_call" | custom-call | tf_op jit(solution)/shard_map/pick/pallas_call | solution.py:420
  45.9 5.5 %collective-permute-start.10 = (f32[3,128,128]{2,1,0:T(8,128)}, f32[3,128,128]{2,1,0:T(8,128)S(1)}, u32[]{:S(2)}, u32[]{:S(2)}) collective-permute-start(f32[3,128,128]{2,1,0:T(8,128)} %pick.1), channel_id=1, source_target_pairs={{0,2},{1,3},{2,4},{3,5},{4,6},{8,10},{9,11},{10,12},{11,13},{12,14... | collective-permute-start | bytes 589832 | tf_op jit(solution)/shard_map/ppermute | solution.py:445
  51.4 1.3 collective-permute-start.11
  52.7 1.9 %collective-permute-start.12 = (f32[3,128,128]{2,1,0:T(8,128)}, f32[3,128,128]{2,1,0:T(8,128)S(1)}, u32[]{:S(2)}, u32[]{:S(2)}) collective-permute-start(f32[3,128,128]{2,1,0:T(8,128)} %pick.1), channel_id=1, source_target_pairs={{0,6},{1,7},{2,0},{3,1},{4,2},{8,14},{9,15},{10,8},{11,9},{12,10},... | collective-permute-start | bytes 589832 | tf_op jit(solution)/shard_map/ppermute | solution.py:445
  54.7 2.3 %col_panel.1.m0 = f32[8,128,128]{2,1,0:T(8,128)} custom-call(s32[2,2,8]{2,1,0:T(2,128)} %pad_add_fusion.pos, f32[8,8,128,128]{3,2,1,0:T(8,128)} %bitcast.32, f32[5,5,128,128]{3,2,1,0:T(8,128)} %get-tuple-element.80.own, f32[1,5,128,128]{3,2,1,0:T(8,128)} %copy-done, f32[4,128,128]{2,1,0:T(8,128)} %copy-done.10), custom_call_target="tpu_custom_call" | custom-call | tf_op jit(solution)/shard_map/col_panel/pallas_call | solution.py:428
  57.0 2.7 %collective-permute-done.11 = f32[3,128,128]{2,1,0:T(8,128)S(1)} collective-permute-done((f32[3,128,128]{2,1,0:T(8,128)}, f32[3,128,128]{2,1,0:T(8,128)S(1)}, u32[]{:S(2)}, u32[]{:S(2)}) %collective-permute-start.11) | collective-permute-done | bytes 196640 | tf_op jit(solution)/shard_map/ppermute | solution.py:445
  59.7 1.9 %collective-permute-done.12 = f32[3,128,128]{2,1,0:T(8,128)S(1)} collective-permute-done((f32[3,128,128]{2,1,0:T(8,128)}, f32[3,128,128]{2,1,0:T(8,128)S(1)}, u32[]{:S(2)}, u32[]{:S(2)}) %collective-permute-start.12) | collective-permute-done | bytes 196640 | tf_op jit(solution)/shard_map/ppermute | solution.py:445
  61.7 1.4 %collective-permute-start.16 = (f32[4,3,128,128]{3,2,1,0:T(8,128)S(1)}, f32[4,3,128,128]{3,2,1,0:T(8,128)S(1)}, u32[]{:S(2)}, u32[]{:S(2)}) collective-permute-start(f32[4,3,128,128]{3,2,1,0:T(8,128)S(1)} %pad_maximum_fusion.mine), channel_id=1, source_target_pairs={{0,1},{1,0},{2,3},{3,2},{4,5},{5,4},{6,7},{7,6},{8,9},{9,8},{10,11... | collective-permute-start | bytes 2359304 | tf_op jit(solution)/shard_map/ppermute | solution.py:453
  63.5 1.4 %collective-permute-start.13 = (f32[8,128,128]{2,1,0:T(8,128)S(1)}, f32[8,128,128]{2,1,0:T(8,128)S(1)}, u32[]{:S(2)}, u32[]{:S(2)}) collective-permute-start(f32[8,128,128]{2,1,0:T(8,128)S(1)} %copy-done.4), channel_id=1, source_target_pairs={{0,2},{1,3},{2,4},{3,5},{4,6},{8,10},{9,11},{10,12},{11,13},{12,14... | collective-permute-start | bytes 1572872 | tf_op jit(solution)/shard_map/ppermute | solution.py:450
  64.9 3.5 %collective-permute-start.14 = (f32[8,128,128]{2,1,0:T(8,128)S(1)}, f32[8,128,128]{2,1,0:T(8,128)S(1)}, u32[]{:S(2)}, u32[]{:S(2)}) collective-permute-start(f32[8,128,128]{2,1,0:T(8,128)S(1)} %copy-done.4), channel_id=1, source_target_pairs={{0,4},{1,5},{2,6},{3,7},{4,0},{8,12},{9,13},{10,14},{11,15},{12,8}... | collective-permute-start | bytes 1572872 | tf_op jit(solution)/shard_map/ppermute | solution.py:450
  68.4 1.9 %collective-permute-start.15 = (f32[8,128,128]{2,1,0:T(8,128)S(1)}, f32[8,128,128]{2,1,0:T(8,128)S(1)}, u32[]{:S(2)}, u32[]{:S(2)}) collective-permute-start(f32[8,128,128]{2,1,0:T(8,128)S(1)} %copy-done.4), channel_id=1, source_target_pairs={{0,6},{1,7},{2,0},{3,1},{4,2},{8,14},{9,15},{10,8},{11,9},{12,10},... | collective-permute-start | bytes 1572872 | tf_op jit(solution)/shard_map/ppermute | solution.py:450
  70.3 3.9 %collective-permute-start.17 = (f32[8,128,128]{2,1,0:T(8,128)S(1)}, f32[8,128,128]{2,1,0:T(8,128)S(1)}, u32[]{:S(2)}, u32[]{:S(2)}) collective-permute-start(f32[8,128,128]{2,1,0:T(8,128)S(1)} %copy-done.4), channel_id=1, source_target_pairs={{0,1},{1,0},{2,3},{3,2},{4,5},{5,4},{6,7},{7,6},{8,9},{9,8},{10,11... | collective-permute-start | bytes 1572872 | tf_op jit(solution)/shard_map/ppermute | solution.py:471
  74.2 14.3 %head.1 = (f32[384,640]{1,0:T(8,128)S(1)}, f32[3,128,128]{2,1,0:T(8,128)S(1)}, f32[256,640]{1,0:T(8,128)S(1)}) custom-call(s32[2]{0:T(128)S(1)} %copy-done.8, f32[4,3,128,128]{3,2,1,0:T(8,128)S(1)} %pad_maximum_fusion.mine, f32[4,3,128,128]{3,2,1,0:T(8,128)S(1)} %collective-permute-done.16.other), custom_call_target="tpu_custom_call" | custom-call | flops 17999998976 | bytes 6000000 | tf_op jit(solution)/shard_map/head/pallas_call | solution.py:454
  88.6 3.3 %collective-permute-done.15.m3 = f32[8,128,128]{2,1,0:T(8,128)S(1)} collective-permute-done((f32[8,128,128]{2,1,0:T(8,128)S(1)}, f32[8,128,128]{2,1,0:T(8,128)S(1)}, u32[]{:S(2)}, u32[]{:S(2)}) %collective-permute-start.15) | collective-permute-done | bytes 524320 | tf_op jit(solution)/shard_map/ppermute | solution.py:450
  91.8 1.6 %collective-permute-start.18 = (f32[8,128,128]{2,1,0:T(8,128)S(1)}, f32[8,128,128]{2,1,0:T(8,128)S(1)}, u32[]{:S(2)}, u32[]{:S(2)}) collective-permute-start(f32[8,128,128]{2,1,0:T(8,128)S(1)} %collective-permute-done.13.m1), channel_id=1, source_target_pairs={{0,1},{1,0},{2,3},{3,2},{4,5},{5,4},{6,7},{7,6},{8,9},{9,8},{10,11... | collective-permute-start | bytes 1572872 | tf_op jit(solution)/shard_map/ppermute | solution.py:471
  93.9 4.4 %middle.1 = (f32[128,640]{1,0:T(8,128)S(1)}, f32[1,128,128]{2,1,0:T(8,128)S(1)}, f32[128,640]{1,0:T(8,128)S(1)}) custom-call(f32[256,640]{1,0:T(8,128)S(1)} %get-tuple-element.56.rest), custom_call_target="tpu_custom_call" | custom-call | flops 6000000000 | bytes 2000000 | tf_op jit(solution)/shard_map/middle/pallas_call | solution.py:472
  98.4 8.0 %tail.1 = (f32[640,640]{1,0:T(8,128)S(1)}, f32[5,128,128]{2,1,0:T(8,128)S(1)}, bf16[1024,640]{1,0:T(8,128)(2,1)S(1)}, bf16[1024,640]{1,0:T(8,128)(2,1)S(1)}, f32[8,128,128]{2,1,0:T(8,128)S(1)}) custom-call(s32[2]{0:T(128)S(1)} %copy-done.8, f32[128,640]{1,0:T(8,128)S(1)} %get-tuple-element.60.rest, f32[384,640]{1,0:T(8,128)S(1)} %get-tuple-element.61.head_inverse, ...), custom_call_target="tpu_custom_call" | custom-call | flops 8999999488 | bytes 6000000 | tf_op jit(solution)/shard_map/tail/pallas_call | solution.py:485
  106.5 1.2 copy-done.2
  107.6 1.1 copy-done.3
  110.5 15.7 %schur.1 = f32[8,8,128,128]{3,2,1,0:T(8,128)} custom-call(s32[2,2,8]{2,1,0:T(2,128)S(1)} %copy-done.7, s32[2]{0:T(128)S(1)} %copy-done.8, f32[8,8,128,128]{3,2,1,0:T(8,128)} %bitcast.33, f32[5,5,128,128]{3,2,1,0:T(8,128)} %get-tuple-element.80.own, f32[1,5,128,128]{3,2,1,0:T(8,128)S(1)} %copy-done.1, f32[4,5,128,128]{3,2,1,0:T(8,128)S(1)} %collective-permute-done.1.below, ...), custom_call_target="tpu_custom_call" | custom-call | tf_op jit(solution)/shard_map/schur/pallas_call | solution.py:508
  (73 shorter events, 8.8 us)
Async XLA Ops:
  6.5 103.0 %all-gather.3.cloned.1.call-start = ((), (), s32[]{:S(2)}) async-start(), calls=%async_computation | async-start | bytes 4718592 | tf_op jit(solution)/shard_map/all_gather | solution.py:419
  7.5 8.4 %collective-permute-start = (f32[1,5,128,128]{3,2,1,0:T(8,128)S(1)}, f32[1,5,128,128]{3,2,1,0:T(8,128)S(1)}, u32[]{:S(2)}, u32[]{:S(2)}) collective-permute-start(f32[1,5,128,128]{3,2,1,0:T(8,128)S(1)} %slice_bitcast_fusion.2), channel_id=1, source_target_pairs={{0,64},{64,0},{128,192},{192,128},{1,65},{65,1},{129,193},{193,129... | collective-permute-start | bytes 983048 | tf_op jit(solution)/shard_map/ppermute | solution.py:381
  18.2 25.1 %collective-permute-start.2 = (f32[4,128,128]{2,1,0:T(8,128)S(1)}, f32[4,128,128]{2,1,0:T(8,128)S(1)}, u32[]{:S(2)}, u32[]{:S(2)}) collective-permute-start(f32[4,128,128]{2,1,0:T(8,128)S(1)} %slice_bitcast_fusion.3), channel_id=1, source_target_pairs={{0,64},{64,0},{128,192},{192,128},{1,65},{65,1},{129,193},{193,129... | collective-permute-start | bytes 786440 | tf_op jit(solution)/shard_map/ppermute | solution.py:396
  20.5 14.9 %collective-permute-start.3 = (f32[128,128]{1,0:T(8,128)}, f32[128,128]{1,0:T(8,128)S(1)}, u32[]{:S(2)}, u32[]{:S(2)}) collective-permute-start(f32[128,128]{1,0:T(8,128)} %tile.1.refs_0_), channel_id=1, source_target_pairs={{0,8},{32,40},{24,32},{9,17},{1,9},{33,41},{18,26},{10,18},{2,10},... | collective-permute-start | bytes 196616 | tf_op jit(solution)/shard_map/ppermute | solution.py:417
  24.2 12.5 %collective-permute-start.4 = (f32[128,128]{1,0:T(8,128)}, f32[128,128]{1,0:T(8,128)S(1)}, u32[]{:S(2)}, u32[]{:S(2)}) collective-permute-start(f32[128,128]{1,0:T(8,128)} %tile.1.refs_0_), channel_id=1, source_target_pairs={{0,16},{32,48},{24,40},{9,25},{1,17},{33,49},{18,34},{10,26},{2,18... | collective-permute-start | bytes 196616 | tf_op jit(solution)/shard_map/ppermute | solution.py:417
  26.9 11.1 %collective-permute-start.5 = (f32[128,128]{1,0:T(8,128)}, f32[128,128]{1,0:T(8,128)S(1)}, u32[]{:S(2)}, u32[]{:S(2)}) collective-permute-start(f32[128,128]{1,0:T(8,128)} %tile.1.refs_0_), channel_id=1, source_target_pairs={{0,24},{32,56},{24,48},{9,33},{1,25},{33,57},{18,42},{10,34},{2,26... | collective-permute-start | bytes 196616 | tf_op jit(solution)/shard_map/ppermute | solution.py:417
  28.9 13.3 %collective-permute-start.6 = (f32[128,128]{1,0:T(8,128)}, f32[128,128]{1,0:T(8,128)S(1)}, u32[]{:S(2)}, u32[]{:S(2)}) collective-permute-start(f32[128,128]{1,0:T(8,128)} %tile.1.refs_0_), channel_id=1, source_target_pairs={{0,32},{32,0},{24,56},{9,41},{1,33},{33,1},{18,50},{10,42},{2,34},... | collective-permute-start | bytes 196616 | tf_op jit(solution)/shard_map/ppermute | solution.py:417
  35.4 6.8 %copy-start.11 = (f32[128,128]{1,0:T(8,128)}, f32[128,128]{1,0:T(8,128)S(1)}, u32[]{:S(2)}) copy-start(f32[128,128]{1,0:T(8,128)S(1)} %collective-permute-done.3.refs_1_) | copy-start | bytes 196612
  35.4 6.9 %collective-permute-start.7 = (f32[128,128]{1,0:T(8,128)}, f32[128,128]{1,0:T(8,128)S(1)}, u32[]{:S(2)}, u32[]{:S(2)}) collective-permute-start(f32[128,128]{1,0:T(8,128)} %tile.1.refs_0_), channel_id=1, source_target_pairs={{0,40},{32,8},{24,0},{9,49},{1,41},{33,9},{18,58},{10,50},{2,42},{... | collective-permute-start | bytes 196616 | tf_op jit(solution)/shard_map/ppermute | solution.py:417
  36.7 5.5 %copy-start.12 = (f32[128,128]{1,0:T(8,128)}, f32[128,128]{1,0:T(8,128)S(1)}, u32[]{:S(2)}) copy-start(f32[128,128]{1,0:T(8,128)S(1)} %collective-permute-done.4.refs_2_) | copy-start | bytes 196612
  36.7 5.6 %collective-permute-start.8 = (f32[128,128]{1,0:T(8,128)}, f32[128,128]{1,0:T(8,128)S(1)}, u32[]{:S(2)}, u32[]{:S(2)}) collective-permute-start(f32[128,128]{1,0:T(8,128)} %tile.1.refs_0_), channel_id=1, source_target_pairs={{0,48},{32,16},{24,8},{9,57},{1,49},{33,17},{18,2},{10,58},{2,50},... | collective-permute-start | bytes 196616 | tf_op jit(solution)/shard_map/ppermute | solution.py:417
  38.1 4.2 %copy-start.13 = (f32[128,128]{1,0:T(8,128)}, f32[128,128]{1,0:T(8,128)S(1)}, u32[]{:S(2)}) copy-start(f32[128,128]{1,0:T(8,128)S(1)} %collective-permute-done.5.refs_3_) | copy-start | bytes 196612
  38.1 5.2 %collective-permute-start.9 = (f32[128,128]{1,0:T(8,128)}, f32[128,128]{1,0:T(8,128)S(1)}, u32[]{:S(2)}, u32[]{:S(2)}) collective-permute-start(f32[128,128]{1,0:T(8,128)} %tile.1.refs_0_), channel_id=1, source_target_pairs={{0,56},{32,24},{24,16},{9,1},{1,57},{33,25},{18,10},{10,2},{2,58},... | collective-permute-start | bytes 196616 | tf_op jit(solution)/shard_map/ppermute | solution.py:417
  42.3 1.7 %copy-start.14 = (f32[128,128]{1,0:T(8,128)}, f32[128,128]{1,0:T(8,128)S(1)}, u32[]{:S(2)}) copy-start(f32[128,128]{1,0:T(8,128)S(1)} %collective-permute-done.6.refs_4_) | copy-start | bytes 196612
  43.3 11.4 %copy-start.10 = (f32[4,128,128]{2,1,0:T(8,128)}, f32[4,128,128]{2,1,0:T(8,128)S(1)}, u32[]{:S(2)}) copy-start(f32[4,128,128]{2,1,0:T(8,128)S(1)} %collective-permute-done.2.below) | copy-start | bytes 786436
  45.9 15.7 %copy-start.9 = (f32[3,128,128]{2,1,0:T(8,128)S(1)}, f32[3,128,128]{2,1,0:T(8,128)}, u32[]{:S(2)}) copy-start(f32[3,128,128]{2,1,0:T(8,128)} %pick.1) | copy-start | bytes 589828
  45.9 11.1 %collective-permute-start.10 = (f32[3,128,128]{2,1,0:T(8,128)}, f32[3,128,128]{2,1,0:T(8,128)S(1)}, u32[]{:S(2)}, u32[]{:S(2)}) collective-permute-start(f32[3,128,128]{2,1,0:T(8,128)} %pick.1), channel_id=1, source_target_pairs={{0,2},{1,3},{2,4},{3,5},{4,6},{8,10},{9,11},{10,12},{11,13},{12,14... | collective-permute-start | bytes 589832 | tf_op jit(solution)/shard_map/ppermute | solution.py:445
  51.4 8.3 %collective-permute-start.11 = (f32[3,128,128]{2,1,0:T(8,128)}, f32[3,128,128]{2,1,0:T(8,128)S(1)}, u32[]{:S(2)}, u32[]{:S(2)}) collective-permute-start(f32[3,128,128]{2,1,0:T(8,128)} %pick.1), channel_id=1, source_target_pairs={{0,4},{1,5},{2,6},{3,7},{4,0},{8,12},{9,13},{10,14},{11,15},{12,8}... | collective-permute-start | bytes 589832 | tf_op jit(solution)/shard_map/ppermute | solution.py:445
  52.7 8.9 %collective-permute-start.12 = (f32[3,128,128]{2,1,0:T(8,128)}, f32[3,128,128]{2,1,0:T(8,128)S(1)}, u32[]{:S(2)}, u32[]{:S(2)}) collective-permute-start(f32[3,128,128]{2,1,0:T(8,128)} %pick.1), channel_id=1, source_target_pairs={{0,6},{1,7},{2,0},{3,1},{4,2},{8,14},{9,15},{10,8},{11,9},{12,10},... | collective-permute-start | bytes 589832 | tf_op jit(solution)/shard_map/ppermute | solution.py:445
  61.7 1.8 %copy-start.4 = (f32[8,128,128]{2,1,0:T(8,128)S(1)}, f32[8,128,128]{2,1,0:T(8,128)}, u32[]{:S(2)}) copy-start(f32[8,128,128]{2,1,0:T(8,128)} %col_panel.1.m0) | copy-start | bytes 1572868
  61.7 12.6 %copy-start.8 = (s32[2]{0:T(128)S(1)}, s32[2]{0:T(128)}, u32[]{:S(2)}) copy-start(s32[2]{0:T(128)} %pad_add_fusion.2.place) | copy-start | bytes 28
  61.7 8.6 %collective-permute-start.16 = (f32[4,3,128,128]{3,2,1,0:T(8,128)S(1)}, f32[4,3,128,128]{3,2,1,0:T(8,128)S(1)}, u32[]{:S(2)}, u32[]{:S(2)}) collective-permute-start(f32[4,3,128,128]{3,2,1,0:T(8,128)S(1)} %pad_maximum_fusion.mine), channel_id=1, source_target_pairs={{0,1},{1,0},{2,3},{3,2},{4,5},{5,4},{6,7},{7,6},{8,9},{9,8},{10,11... | collective-permute-start | bytes 2359304 | tf_op jit(solution)/shard_map/ppermute | solution.py:453
  63.2 35.1 %collective-permute-start.1 = (f32[4,5,128,128]{3,2,1,0:T(8,128)S(1)}, f32[4,5,128,128]{3,2,1,0:T(8,128)S(1)}, u32[]{:S(2)}, u32[]{:S(2)}) collective-permute-start(f32[4,5,128,128]{3,2,1,0:T(8,128)S(1)} %slice.23), channel_id=1, source_target_pairs={{0,64},{64,0},{128,192},{192,128},{1,65},{65,1},{129,193},{193,129... | collective-permute-start | bytes 3932168 | tf_op jit(solution)/shard_map/ppermute | solution.py:397
  63.5 25.1 %collective-permute-start.13 = (f32[8,128,128]{2,1,0:T(8,128)S(1)}, f32[8,128,128]{2,1,0:T(8,128)S(1)}, u32[]{:S(2)}, u32[]{:S(2)}) collective-permute-start(f32[8,128,128]{2,1,0:T(8,128)S(1)} %copy-done.4), channel_id=1, source_target_pairs={{0,2},{1,3},{2,4},{3,5},{4,6},{8,10},{9,11},{10,12},{11,13},{12,14... | collective-permute-start | bytes 1572872 | tf_op jit(solution)/shard_map/ppermute | solution.py:450
  64.9 23.7 %collective-permute-start.14 = (f32[8,128,128]{2,1,0:T(8,128)S(1)}, f32[8,128,128]{2,1,0:T(8,128)S(1)}, u32[]{:S(2)}, u32[]{:S(2)}) collective-permute-start(f32[8,128,128]{2,1,0:T(8,128)S(1)} %copy-done.4), channel_id=1, source_target_pairs={{0,4},{1,5},{2,6},{3,7},{4,0},{8,12},{9,13},{10,14},{11,15},{12,8}... | collective-permute-start | bytes 1572872 | tf_op jit(solution)/shard_map/ppermute | solution.py:450
  68.4 23.4 %collective-permute-start.15 = (f32[8,128,128]{2,1,0:T(8,128)S(1)}, f32[8,128,128]{2,1,0:T(8,128)S(1)}, u32[]{:S(2)}, u32[]{:S(2)}) collective-permute-start(f32[8,128,128]{2,1,0:T(8,128)S(1)} %copy-done.4), channel_id=1, source_target_pairs={{0,6},{1,7},{2,0},{3,1},{4,2},{8,14},{9,15},{10,8},{11,9},{12,10},... | collective-permute-start | bytes 1572872 | tf_op jit(solution)/shard_map/ppermute | solution.py:450
  70.3 28.0 %collective-permute-start.17 = (f32[8,128,128]{2,1,0:T(8,128)S(1)}, f32[8,128,128]{2,1,0:T(8,128)S(1)}, u32[]{:S(2)}, u32[]{:S(2)}) collective-permute-start(f32[8,128,128]{2,1,0:T(8,128)S(1)} %copy-done.4), channel_id=1, source_target_pairs={{0,1},{1,0},{2,3},{3,2},{4,5},{5,4},{6,7},{7,6},{8,9},{9,8},{10,11... | collective-permute-start | bytes 1572872 | tf_op jit(solution)/shard_map/ppermute | solution.py:471
  91.8 6.5 %collective-permute-start.18 = (f32[8,128,128]{2,1,0:T(8,128)S(1)}, f32[8,128,128]{2,1,0:T(8,128)S(1)}, u32[]{:S(2)}, u32[]{:S(2)}) collective-permute-start(f32[8,128,128]{2,1,0:T(8,128)S(1)} %collective-permute-done.13.m1), channel_id=1, source_target_pairs={{0,1},{1,0},{2,3},{3,2},{4,5},{5,4},{6,7},{7,6},{8,9},{9,8},{10,11... | collective-permute-start | bytes 1572872 | tf_op jit(solution)/shard_map/ppermute | solution.py:471
  93.4 5.0 %collective-permute-start.19 = (f32[8,128,128]{2,1,0:T(8,128)S(1)}, f32[8,128,128]{2,1,0:T(8,128)S(1)}, u32[]{:S(2)}, u32[]{:S(2)}) collective-permute-start(f32[8,128,128]{2,1,0:T(8,128)S(1)} %collective-permute-done.14.m2), channel_id=1, source_target_pairs={{0,1},{1,0},{2,3},{3,2},{4,5},{5,4},{6,7},{7,6},{8,9},{9,8},{10,11... | collective-permute-start | bytes 1572872 | tf_op jit(solution)/shard_map/ppermute | solution.py:471
  93.4 5.0 %collective-permute-start.20 = (f32[8,128,128]{2,1,0:T(8,128)S(1)}, f32[8,128,128]{2,1,0:T(8,128)S(1)}, u32[]{:S(2)}, u32[]{:S(2)}) collective-permute-start(f32[8,128,128]{2,1,0:T(8,128)S(1)} %collective-permute-done.15.m3), channel_id=1, source_target_pairs={{0,1},{1,0},{2,3},{3,2},{4,5},{5,4},{6,7},{7,6},{8,9},{9,8},{10,11... | collective-permute-start | bytes 1572872 | tf_op jit(solution)/shard_map/ppermute | solution.py:471
  98.4 11.1 %copy-start.1 = (f32[1,5,128,128]{3,2,1,0:T(8,128)S(1)}, f32[1,5,128,128]{3,2,1,0:T(8,128)}, u32[]{:S(2)}) copy-start(f32[1,5,128,128]{3,2,1,0:T(8,128)} %copy-done) | copy-start | bytes 983044
  98.4 11.1 %copy-start.7 = (s32[2,2,8]{2,1,0:T(2,128)S(1)}, s32[2,2,8]{2,1,0:T(2,128)}, u32[]{:S(2)}) copy-start(s32[2,2,8]{2,1,0:T(2,128)} %pad_add_fusion.pos) | copy-start | bytes 388
  (8 other events, 8.7 us)
Sparse Core Ops, SparseCore 0:
  43.4 56.3 all-gather.2
